TPU v7x, 256 devices: a whole 4x4x8 slice. The times are simulated.
256 devices in a mesh: lat: 8 (over z), lon: 32 (over x, y, core).
Axes of the slice: x: 4, y: 4, z: 8, core: 2. Of those that a mesh axis runs over, the one named last changes fastest.
Arguments:
- ensemble: float32 [256, 512, 8, 256], P('lat', 'lon'), may hold values from -6 to 6
- obs_values: float32 [3, 256], replicated, may hold values from -8 to 8
- obs_noise: float32 [3, 256, 256], replicated, may hold values from -6 to 6
- obs_var: float32 [3, 256], replicated, may hold values from 0.1 to 1
- obs_cells: int32 [3, 256], replicated, may hold values from 0 to 4095, as said below
- owner_tiles: int32 [3, 2], replicated, may hold values from 0 to 31, as said below
- radius: int32 [3], replicated, may hold values from 64 to 128, as said below
- courant_lat: float32 [256, 512, 8], P('lat', 'lon'), may hold values from -0.35 to 0.35
- courant_lon: float32 [256, 512, 8], P('lat', 'lon'), may hold values from -0.35 to 0.35
- diffusivity: float32 [256, 512, 8], P('lat', 'lon'), may hold values from 0.02 to 0.07
Outputs:
- forecast: float32 [256, 512, 8, 256], P('lat', 'lon')
Inputs may be any that keep to these rules, and one draw needn't show every extreme that they name: `obs_cells`: each row holds 256 distinct local cells, the last cell of the tile among them; cell (i, j, k) of a tile has index (i * 16 + j) * 8 + k. `owner_tiles`: row b names a latitude tile below 8 and a longitude tile below 32; consecutive batches' tiles differ by at most one in each (longitude wraps). `radius`: every draw holds both ends.
All inputs are finite; a program needn't handle non-finite values.
Results may differ from a plain program's by a relative error of at most 0.0003.
Values sent between devices are 32-bit elements; how exact they have to be, the bound alone decides.
A program may use at most 64 MiB of HBM per device.

v0:
```python
import jax
import jax.numpy as jnp
from jax import lax
from jax.sharding import Mesh
from jax.sharding import PartitionSpec as P

LEV = 8
NBATCH = 3
CLAT = 32
CLON = 16
LON = ("lon_0", "lon_1", "lon_2")


def in_blocks(x, dim, size):
    dims = x.shape
    tiles = x.reshape(*dims[:dim], size, dims[dim] // size, *dims[dim + 1 :])
    return jnp.moveaxis(tiles, dim, 0)


def sent_and_summed(x, axis, dim):
    tiles = in_blocks(x, dim, lax.axis_size(axis))
    arrived = lax.all_to_all(tiles, axis, split_axis=0, concat_axis=0, tiled=True)
    return arrived.sum(axis=0)


def summed_rows(x, axes, dim):
    far, near = axes
    tiles = in_blocks(x, dim, lax.axis_size(far))
    nearer = sent_and_summed(tiles, near, dim + 1)
    arrived = lax.all_to_all(nearer, far, split_axis=0, concat_axis=0, tiled=True)
    return arrived.sum(axis=0)


def filled_up(lines, size):
    spare = -len(lines) % size
    return jnp.pad(lines, [(0, spare)] + [(0, 0)] * (lines.ndim - 1))


def sent_to_all(x, axis):
    size = lax.axis_size(axis)
    return lax.all_to_all(jnp.broadcast_to(x[None], (size, *x.shape)), axis, 0, 0, tiled=True)


def laid_out(tiles, dim):
    dims = list(tiles.shape[1:])
    dims[dim] *= tiles.shape[0]
    return jnp.moveaxis(tiles, 0, dim).reshape(dims)


def whole_of(x, axes, dim):
    far, near = axes
    first = sent_to_all(x, far)
    tiles = jnp.swapaxes(sent_to_all(first, near), 0, 1)
    return laid_out(tiles.reshape(-1, *x.shape), dim)


def total_of(x, axes):
    lines = x.reshape(-1, x.shape[-1])
    own = summed_rows(filled_up(lines, lax.axis_size(axes[0]) * lax.axis_size(axes[1])), axes, 0)
    whole = whole_of(own, axes, 0)
    return whole[: len(lines)].reshape(x.shape)


def extended(x, sides, width, wrap):
    for axis, dim in sides:
        size, length = (lax.axis_size(axis), x.shape[dim])
        up = [(i, (i + 1) % size) for i in range(size if wrap else size - 1)]
        down = [(j, i) for i, j in up]
        last = lax.slice_in_dim(x, length - width, length, axis=dim)
        first = lax.slice_in_dim(x, 0, width, axis=dim)
        before = lax.ppermute(last, axis, up)
        after = lax.ppermute(first, axis, down)
        x = jnp.concatenate([before, x, after], axis=dim)
    return x


def taper_weight(dist_sq, radius_cells):
    ratio = 1.0 - dist_sq / (radius_cells * radius_cells)
    return jnp.square(jnp.maximum(ratio, 0.0))


def analysis(observed_rows, values, noise, variance):
    members = observed_rows.shape[1]
    spread = observed_rows - jnp.mean(observed_rows, axis=1, keepdims=True)
    covariance = jnp.dot(spread, spread.T, precision=lax.Precision.HIGHEST) / (
        members - 1
    ) + jnp.diag(variance)
    innovation = values[:, None] + jnp.sqrt(variance)[:, None] * noise - observed_rows
    factor = jnp.linalg.cholesky(covariance)
    inner = jax.scipy.linalg.solve_triangular(factor, innovation, lower=True)
    weights = jax.scipy.linalg.solve_triangular(factor, inner, lower=True, trans=1)
    return (spread, weights)


def locality(lat_cells, lon_cells, cells, owner_lat, owner_lon, radius_cells, total_lon):
    position = cells // LEV
    obs_lat = owner_lat * CLAT + position // CLON
    obs_lon = owner_lon * CLON + position % CLON
    lat_gap = (lat_cells[:, None] - obs_lat[None, :]).astype(jnp.float32)
    lon_gap = jnp.abs(lon_cells[:, None] - obs_lon[None, :])
    lon_gap = jnp.minimum(lon_gap, total_lon - lon_gap).astype(jnp.float32)
    dist_sq = jnp.square(lat_gap) + jnp.square(lon_gap)
    return taper_weight(dist_sq, radius_cells.astype(jnp.float32))


def regress(flat_state, spread, weights, weight_map):
    members = flat_state.shape[1]
    places = weight_map.shape[0]
    levels = flat_state.shape[0] // places
    anomaly = flat_state - jnp.mean(flat_state, axis=1, keepdims=True)
    covar = jnp.dot(anomaly, spread.T, precision=lax.Precision.HIGHEST) / (members - 1)
    covar = (covar.reshape(places, levels, -1) * weight_map[:, None, :]).reshape(covar.shape)
    return flat_state + jnp.dot(covar, weights, precision=lax.Precision.HIGHEST)


def advance(padded, lat_speed, lon_speed, spread_rate):
    centre = padded[1:-1, 1:-1]
    below_row = padded[:-2, 1:-1]
    above_row = padded[2:, 1:-1]
    west_col = padded[1:-1, :-2]
    east_col = padded[1:-1, 2:]
    lat_part = lat_speed[..., None]
    lon_part = lon_speed[..., None]
    rate_part = spread_rate[..., None]
    transport = (
        jnp.maximum(lat_part, 0.0) * (centre - below_row)
        + jnp.minimum(lat_part, 0.0) * (above_row - centre)
        + jnp.maximum(lon_part, 0.0) * (centre - west_col)
        + jnp.minimum(lon_part, 0.0) * (east_col - centre)
    )
    return (
        centre
        - transport
        + rate_part * (below_row + above_row + west_col + east_col - 4.0 * centre)
    )


def shards(
    ensemble,
    obs_values,
    obs_noise,
    obs_var,
    obs_cells,
    owner_tiles,
    radius,
    courant_lat,
    courant_lon,
    diffusivity,
):
    lat_index = lax.axis_index("lat")
    lon_index = lax.axis_index(LON)
    lon_count = lax.axis_size(LON)
    total_lon = CLON * lon_count
    members = ensemble.shape[3]
    lat_cells = jnp.broadcast_to(
        (lat_index * CLAT + jnp.arange(CLAT, dtype=jnp.int32))[:, None], (CLAT, CLON)
    ).reshape(-1)
    lon_cells = jnp.broadcast_to(
        (lon_index * CLON + jnp.arange(CLON, dtype=jnp.int32))[None, :], (CLAT, CLON)
    ).reshape(-1)
    flat_state = ensemble.reshape(-1, members)
    for which_batch in range(NBATCH):
        owner_lat = owner_tiles[which_batch, 0]
        owner_lon = owner_tiles[which_batch, 1]
        picked = flat_state[obs_cells[which_batch]]
        is_owner = jnp.logical_and(lat_index == owner_lat, lon_index == owner_lon)
        observed_rows = total_of(
            jnp.where(is_owner, picked, 0.0), (("lat", "lon_0"), ("lon_1", "lon_2"))
        )
        spread, weights = analysis(
            observed_rows, obs_values[which_batch], obs_noise[which_batch], obs_var[which_batch]
        )
        weight_map = locality(
            lat_cells,
            lon_cells,
            obs_cells[which_batch],
            owner_lat,
            owner_lon,
            radius[which_batch],
            total_lon,
        )
        flat_state = regress(flat_state, spread, weights, weight_map)
    state = flat_state.reshape(ensemble.shape)
    widened = extended(state, (("lat", 0),), 2, False)
    widened = extended(widened, ((LON, 1),), 2, True)
    stacked = jnp.stack([courant_lat, courant_lon, diffusivity])
    stacked = extended(stacked, (("lat", 1),), 1, False)
    stacked = extended(stacked, ((LON, 2),), 1, True)
    middle = advance(widened, stacked[0], stacked[1], stacked[2])
    state = advance(middle, courant_lat, courant_lon, diffusivity)
    return state


def solution(mesh):
    split = Mesh(
        mesh.devices.reshape(mesh.shape["lat"], 4, 4, 2), ("lat", "lon_0", "lon_1", "lon_2")
    )
    return jax.shard_map(
        shards,
        mesh=split,
        in_specs=(
            P("lat", LON, None, None),
            P(),
            P(),
            P(),
            P(),
            P(),
            P(),
            P("lat", LON, None),
            P("lat", LON, None),
            P("lat", LON, None),
        ),
        out_specs=P("lat", LON, None, None),
        check_vma=False,
    )
```

profile of v0, /device:TPU:1, one launch (start us, length us, event | category | flops | bytes accessed | tf_op | source)
XLA Modules:
  0.0 442.4 jit_solution(11629982724466620871)
XLA Ops:
  0.0 1.6 fusion.108
  2.4 3.2 gather_fusion
  7.8 6.6 %all-to-all-start = ((f32[8,32,1,256]{3,1,2,0:T(8,128)}), f32[8,32,1,256]{3,1,2,0:T(8,128)S(1)}, u32[]{:S(2)}, u32[]{:S(2)}) async-start(f32[8,32,1,256]{3,1,2,0:T(8,128)} %copy.85), calls=%async_computation | async-start | bytes 524288 | tf_op jit(solution)/shard_map/all_to_all | solution.py:22
  20.7 2.8 reduce_sum.114
  23.6 4.0 broadcast_subtract_fusion
  27.7 0.9 fusion.30
  29.3 10.5 %all-to-all-start.1 = ((f32[32,1,256]{2,1,0:T(1,128)}), f32[32,1,256]{2,1,0:T(1,128)S(1)}, u32[]{:S(2)}, u32[]{:S(2)}) async-start(f32[32,1,256]{2,1,0:T(1,128)} %reduce_sum.116), calls=%async_computation.1 | async-start | bytes 65536 | tf_op jit(solution)/shard_map/all_to_all | solution.py:30
  39.8 8.8 %all-to-all-done.1 = f32[32,1,256]{2,1,0:T(1,128)S(1)} async-done(((f32[32,1,256]{2,1,0:T(1,128)}), f32[32,1,256]{2,1,0:T(1,128)S(1)}, u32[]{:S(2)}, u32[]{:S(2)}) %all-to-all-start.1) | async-done | bytes 32800 | tf_op jit(solution)/shard_map/all_to_all | solution.py:30
  49.3 3.8 all-to-all-start.2
  53.1 8.6 %all-to-all-done.2 = f32[32,1,256]{2,1,0:T(1,128)S(1)} async-done(((f32[32,1,256]{2,1,0:T(1,128)}), f32[32,1,256]{2,1,0:T(1,128)S(1)}, u32[]{:S(2)}, u32[]{:S(2)}) %all-to-all-start.2) | async-done | bytes 32800 | tf_op jit(solution)/shard_map/all_to_all | solution.py:41
  62.5 7.7 %all-to-all-start.3 = ((f32[8,32,1,256]{3,1,2,0:T(8,128)}), f32[8,32,1,256]{3,1,2,0:T(8,128)S(1)}, u32[]{:S(2)}, u32[]{:S(2)}) async-start(f32[8,32,1,256]{3,1,2,0:T(8,128)} %broadcast_in_dim.68), calls=%async_computation.3 | async-start | bytes 524288 | tf_op jit(solution)/shard_map/all_to_all | solution.py:41
  71.4 5.2 %all-to-all-done.3 = f32[8,32,1,256]{3,1,2,0:T(8,128)S(1)} async-done(((f32[8,32,1,256]{3,1,2,0:T(8,128)}), f32[8,32,1,256]{3,1,2,0:T(8,128)S(1)}, u32[]{:S(2)}, u32[]{:S(2)}) %all-to-all-start.3) | async-done | bytes 262176 | tf_op jit(solution)/shard_map/all_to_all | solution.py:41
  77.7 11.7 %cholesky.172 = f32[128,128]{1,0:T(8,128)S(1)} custom-call(f32[128,128]{1,0:T(8,128)S(1)} %cholesky.270), custom_call_target="Cholesky" | custom-call | tf_op jit(solution)/shard_map/jit(cholesky)/cholesky | solution.py:89
  89.5 9.8 %custom-call.20 = f32[1,128,128]{1,2,0:T(8,128)S(1)} custom-call(f32[1,128,128]{2,1,0:T(8,128)S(1)} %get-tuple-element.118), custom_call_target="InvertDiagBlocksLowerTriangular" | custom-call | tf_op jit(solution)/shard_map/jit(cholesky)/cholesky | solution.py:89
  99.8 11.7 %cholesky.189 = f32[128,128]{1,0:T(8,128)S(1)} custom-call(f32[128,128]{1,0:T(8,128)S(1)} %convolution_subtract_fusion.8), custom_call_target="Cholesky" | custom-call | tf_op jit(solution)/shard_map/jit(cholesky)/cholesky | solution.py:89
  113.5 3.8 while.12
  114.1 1.3 bitcast_dynamic-update-slice_fusion.6
  116.0 1.3 bitcast_dynamic-update-slice_fusion.6
  117.3 19.8 %custom-call.22 = f32[2,128,128]{1,2,0:T(8,128)S(1)} custom-call(f32[2,128,128]{2,1,0:T(8,128)S(1)} %get-tuple-element.49), custom_call_target="InvertDiagBlocksLowerTriangular" | custom-call | tf_op jit(solution)/shard_map/jit(_solve_triangular)/triangular_solve | solution.py:91
  139.1 6.0 %fusion.2 = f32[4096,256]{1,0:T(8,128)S(1)} fusion(f32[4096,256]{1,0:T(8,128)} %bitcast.267, f32[512,256]{1,0:T(8,128)S(1)} %get-tuple-element.130, f32[8,32,1,256]{3,1,2,0:T(8,128)S(1)} %all-to-all-done.3, f32[32,8]{1,0:T(8,128)S(1)} %broadcast_multiply_fusion.5), kind=kOutput, calls=%fused_computation.18 | convolution fusion | flops 3223388160 | bytes 9176064 | tf_op jit(solution)/shard_map/dot_general | solution.py:111
  145.1 5.1 %fusion.110 = (f32[4096]{0:T(1024)S(1)}, f32[4096,256]{1,0:T(8,128)}) fusion(f32[4096,256]{1,0:T(8,128)S(1)} %bitcast.266, f32[4096,256]{1,0:T(8,128)S(1)} %fusion.2, f32[128,256]{1,0:T(8,128)S(1)} %fusion.79, f32[128,256]{1,0:T(8,128)S(1)} %fusion.77), kind=kOutput, calls=%fused_computation.268 | convolution fusion | flops 3223384064 | bytes 12861440 | tf_op jit(solution)/shard_map/dot_general | solution.py:113
  150.3 3.2 gather_fusion.1
  153.8 9.9 %all_to_all.62 = f32[8,32,1,256]{3,1,2,0:T(8,128)S(1)} all-to-all(f32[8,32,1,256]{3,1,2,0:T(8,128)S(1)} %copy.91), channel_id=1, replica_groups=mesh['lat'=8,'lon_0'=4,'lon_1'=4,'lon_2'=2] {'lon_1','lon_2'}, dimensions={0} | all-to-all | bytes 524288 | tf_op jit(solution)/shard_map/all_to_all | solution.py:22
  163.8 11.6 %all_to_all.63 = f32[32,1,256]{2,1,0:T(1,128)S(1)} all-to-all(f32[32,1,256]{2,1,0:T(1,128)S(1)} %reduce_sum.121), channel_id=1, replica_groups=mesh['lat'=8,'lon_0'=4,'lon_1'=4,'lon_2'=2] {'lat','lon_0'}, dimensions={0} | all-to-all | bytes 65536 | tf_op jit(solution)/shard_map/all_to_all | solution.py:30
  175.5 11.7 %all_to_all.60 = f32[32,1,256]{2,1,0:T(1,128)S(1)} all-to-all(f32[32,1,256]{2,1,0:T(1,128)S(1)} %broadcast_in_dim.129), channel_id=1, replica_groups=mesh['lat'=8,'lon_0'=4,'lon_1'=4,'lon_2'=2] {'lat','lon_0'}, dimensions={0} | all-to-all | bytes 65536 | tf_op jit(solution)/shard_map/all_to_all | solution.py:41
  187.9 6.9 %all-to-all-start.7 = ((f32[8,32,1,256]{3,1,2,0:T(8,128)}), f32[8,32,1,256]{3,1,2,0:T(8,128)S(1)}, u32[]{:S(2)}, u32[]{:S(2)}) async-start(f32[8,32,1,256]{3,1,2,0:T(8,128)} %broadcast_in_dim.131), calls=%async_computation.7 | async-start | bytes 524288 | tf_op jit(solution)/shard_map/all_to_all | solution.py:41
  196.1 5.2 %all-to-all-done.7 = f32[8,32,1,256]{3,1,2,0:T(8,128)S(1)} async-done(((f32[8,32,1,256]{3,1,2,0:T(8,128)}), f32[8,32,1,256]{3,1,2,0:T(8,128)S(1)}, u32[]{:S(2)}, u32[]{:S(2)}) %all-to-all-start.7) | async-done | bytes 262176 | tf_op jit(solution)/shard_map/all_to_all | solution.py:41
  202.4 11.7 %cholesky.206 = f32[128,128]{1,0:T(8,128)S(1)} custom-call(f32[128,128]{1,0:T(8,128)S(1)} %cholesky.273), custom_call_target="Cholesky" | custom-call | tf_op jit(solution)/shard_map/jit(cholesky)/cholesky | solution.py:89
  214.2 9.8 %custom-call.23 = f32[1,128,128]{1,2,0:T(8,128)S(1)} custom-call(f32[1,128,128]{2,1,0:T(8,128)S(1)} %get-tuple-element.114), custom_call_target="InvertDiagBlocksLowerTriangular" | custom-call | tf_op jit(solution)/shard_map/jit(cholesky)/cholesky | solution.py:89
  224.5 11.7 %cholesky.223 = f32[128,128]{1,0:T(8,128)S(1)} custom-call(f32[128,128]{1,0:T(8,128)S(1)} %convolution_subtract_fusion.7), custom_call_target="Cholesky" | custom-call | tf_op jit(solution)/shard_map/jit(cholesky)/cholesky | solution.py:89
  238.9 4.0 while.13
  239.6 1.4 bitcast_dynamic-update-slice_fusion.7
  241.6 1.4 bitcast_dynamic-update-slice_fusion.7
  242.9 20.1 %custom-call.25 = f32[2,128,128]{1,2,0:T(8,128)S(1)} custom-call(f32[2,128,128]{2,1,0:T(8,128)S(1)} %get-tuple-element.51), custom_call_target="InvertDiagBlocksLowerTriangular" | custom-call | tf_op jit(solution)/shard_map/jit(_solve_triangular)/triangular_solve | solution.py:91
  265.0 6.1 %fusion.1 = f32[4096,256]{1,0:T(8,128)S(1)} fusion(f32[4096,256]{1,0:T(8,128)} %get-tuple-element.147, f32[512,256]{1,0:T(8,128)S(1)} %get-tuple-element.129, f32[4096]{0:T(1024)S(1)} %broadcast_multiply_fusion.2, f32[8,32,1,256]{3,1,2,0:T(8,128)S(1)} %all-to-all-done.7, f32[256]{0:T(256)S(1)} %div.146), kind=kOutput, calls=%fused_computation.15 | convolution fusion | flops 3224436736 | bytes 9192448 | tf_op jit(solution)/shard_map/dot_general | solution.py:111
  271.1 5.1 %fusion.111 = (f32[4096]{0:T(1024)S(1)}, f32[4096,256]{1,0:T(8,128)}) fusion(f32[4096,256]{1,0:T(8,128)S(1)} %copy-done.2, f32[4096,256]{1,0:T(8,128)S(1)} %fusion.1, f32[128,256]{1,0:T(8,128)S(1)} %fusion.82, f32[128,256]{1,0:T(8,128)S(1)} %fusion.80), kind=kOutput, calls=%fused_computation.269 | convolution fusion | flops 3223384064 | bytes 12861440 | tf_op jit(solution)/shard_map/dot_general | solution.py:113
  276.2 3.2 gather_fusion.2
  279.8 9.9 %all_to_all.64 = f32[8,32,1,256]{3,1,2,0:T(8,128)S(1)} all-to-all(f32[8,32,1,256]{3,1,2,0:T(8,128)S(1)} %copy.97), channel_id=1, replica_groups=mesh['lat'=8,'lon_0'=4,'lon_1'=4,'lon_2'=2] {'lon_1','lon_2'}, dimensions={0} | all-to-all | bytes 524288 | tf_op jit(solution)/shard_map/all_to_all | solution.py:22
  289.8 11.6 %all_to_all.65 = f32[32,1,256]{2,1,0:T(1,128)S(1)} all-to-all(f32[32,1,256]{2,1,0:T(1,128)S(1)} %reduce_sum.126), channel_id=1, replica_groups=mesh['lat'=8,'lon_0'=4,'lon_1'=4,'lon_2'=2] {'lat','lon_0'}, dimensions={0} | all-to-all | bytes 65536 | tf_op jit(solution)/shard_map/all_to_all | solution.py:30
  301.5 11.7 %all_to_all.61 = f32[32,1,256]{2,1,0:T(1,128)S(1)} all-to-all(f32[32,1,256]{2,1,0:T(1,128)S(1)} %broadcast_in_dim.134), channel_id=1, replica_groups=mesh['lat'=8,'lon_0'=4,'lon_1'=4,'lon_2'=2] {'lat','lon_0'}, dimensions={0} | all-to-all | bytes 65536 | tf_op jit(solution)/shard_map/all_to_all | solution.py:41
  313.9 6.8 %all-to-all-start.11 = ((f32[8,32,1,256]{3,1,2,0:T(8,128)}), f32[8,32,1,256]{3,1,2,0:T(8,128)S(1)}, u32[]{:S(2)}, u32[]{:S(2)}) async-start(f32[8,32,1,256]{3,1,2,0:T(8,128)} %broadcast_in_dim.136), calls=%async_computation.11 | async-start | bytes 524288 | tf_op jit(solution)/shard_map/all_to_all | solution.py:41
  320.8 6.4 %all-to-all-done.11 = f32[8,32,1,256]{3,1,2,0:T(8,128)S(1)} async-done(((f32[8,32,1,256]{3,1,2,0:T(8,128)}), f32[8,32,1,256]{3,1,2,0:T(8,128)S(1)}, u32[]{:S(2)}, u32[]{:S(2)}) %all-to-all-start.11) | async-done | bytes 262176 | tf_op jit(solution)/shard_map/all_to_all | solution.py:41
  328.4 11.7 %cholesky.240 = f32[128,128]{1,0:T(8,128)S(1)} custom-call(f32[128,128]{1,0:T(8,128)S(1)} %cholesky.276), custom_call_target="Cholesky" | custom-call | tf_op jit(solution)/shard_map/jit(cholesky)/cholesky | solution.py:89
  340.1 9.8 %custom-call.26 = f32[1,128,128]{1,2,0:T(8,128)S(1)} custom-call(f32[1,128,128]{2,1,0:T(8,128)S(1)} %get-tuple-element.110), custom_call_target="InvertDiagBlocksLowerTriangular" | custom-call | tf_op jit(solution)/shard_map/jit(cholesky)/cholesky | solution.py:89
  350.4 11.7 %cholesky.257 = f32[128,128]{1,0:T(8,128)S(1)} custom-call(f32[128,128]{1,0:T(8,128)S(1)} %convolution_subtract_fusion.6), custom_call_target="Cholesky" | custom-call | tf_op jit(solution)/shard_map/jit(cholesky)/cholesky | solution.py:89
  364.9 4.0 while.14
  365.5 1.4 bitcast_dynamic-update-slice_fusion.8
  367.5 1.4 bitcast_dynamic-update-slice_fusion.8
  368.9 19.9 %custom-call.28 = f32[2,128,128]{1,2,0:T(8,128)S(1)} custom-call(f32[2,128,128]{2,1,0:T(8,128)S(1)} %get-tuple-element.53), custom_call_target="InvertDiagBlocksLowerTriangular" | custom-call | tf_op jit(solution)/shard_map/jit(_solve_triangular)/triangular_solve | solution.py:91
  390.7 5.8 %fusion = f32[4096,256]{1,0:T(8,128)S(1)} fusion(f32[4096,256]{1,0:T(8,128)} %get-tuple-element.151, f32[512,256]{1,0:T(8,128)S(1)} %get-tuple-element.128, f32[4096]{0:T(1024)S(1)} %broadcast_multiply_fusion.1, f32[8,32,1,256]{3,1,2,0:T(8,128)S(1)} %all-to-all-done.11, f32[256]{0:T(256)S(1)} %div.159), kind=kOutput, calls=%fused_computation.12 | convolution fusion | flops 3224436736 | bytes 9192448 | tf_op jit(solution)/shard_map/dot_general | solution.py:111
  396.5 3.4 convolution_add_fusion
  400.0 2.3 collective-permute-start
  402.4 1.3 collective-permute-start.1
  403.8 4.0 collective-permute-start.4
  407.8 1.3 collective-permute-start.5
  409.1 1.6 collective-permute-done.1
  410.7 1.1 pad_maximum_fusion.9
  411.9 2.5 collective-permute-start.2
  414.5 3.3 collective-permute-start.6
  417.8 2.0 collective-permute-start.7
  425.6 1.0 copy.105
  426.7 2.8 pad_maximum_fusion
  430.2 6.4 %multiply_add_fusion = f32[34,18,8,256]{3,2,1,0:T(8,128)S(1)} fusion(f32[36,2,8,256]{3,2,1,0:T(8,128)S(1)} %collective-permute-done.3, f32[2,16,8,256]{3,2,1,0:T(8,128)S(1)} %collective-permute-done.1, f32[32,16,8,256]{3,2,1,0:T(8,128)S(1)} %bitcast.264, f32[2,16,8,256]{3,2,1,0:T(8,128)S(1)} %collective-permute-done, ...), kind=kLoop, calls=%fused_computation.25 | loop fusion | flops 31334400 | bytes 26050176 | tf_op jit(solution)/shard_map/add | solution.py:132
  436.7 5.4 %multiply_add_fusion.1 = f32[32,16,8,256]{3,2,1,0:T(8,128)} fusion(f32[34,18,8,256]{3,2,1,0:T(8,128)S(1)} %multiply_add_fusion, f32[32,16,8]{2,1,0:T(8,128)S(1)} %copy-done.6, f32[32,16,8]{2,1,0:T(8,128)S(1)} %copy-done.10, f32[32,16,8]{2,1,0:T(8,128)S(1)} %copy-done.9, f32[32,16,8]{2,1,0:T(8,128)S(1)} %copy-done.8, f32[32,16,8]{2,1,0:T(8,128)S(1)} %copy-done.7), kind=kLoop, calls=%fused_computation.26 | loop fusion | flops 19922944 | bytes 25247744 | tf_op jit(solution)/shard_map/add | solution.py:132
  (197 shorter events, 32.1 us)
Async XLA Ops:
  0.0 18.3 %copy-start.16 = (s32[3]{0:T(128)S(1)}, s32[3]{0:T(128)}, u32[]{:S(2)}) copy-start(s32[3]{0:T(128)} %param.21) | copy-start | bytes 40
  7.8 20.8 %all-to-all-start = ((f32[8,32,1,256]{3,1,2,0:T(8,128)}), f32[8,32,1,256]{3,1,2,0:T(8,128)S(1)}, u32[]{:S(2)}, u32[]{:S(2)}) async-start(f32[8,32,1,256]{3,1,2,0:T(8,128)} %copy.85), calls=%async_computation | async-start | bytes 524288 | tf_op jit(solution)/shard_map/all_to_all | solution.py:22
  23.6 4.0 copy-start.15
  23.6 16.2 %copy-start.17 = (f32[3,256]{1,0:T(4,128)S(1)}, f32[3,256]{1,0:T(4,128)}, u32[]{:S(2)}) copy-start(f32[3,256]{1,0:T(4,128)} %param.18) | copy-start | bytes 9220
  23.6 47.8 %copy-start.18 = (f32[3,256]{1,0:T(4,128)S(1)}, f32[3,256]{1,0:T(4,128)}, u32[]{:S(2)}) copy-start(f32[3,256]{1,0:T(4,128)} %param.16) | copy-start | bytes 9220
  27.6 109.6 %copy-start.14 = (f32[3,256,256]{2,1,0:T(8,128)S(1)}, f32[3,256,256]{2,1,0:T(8,128)}, u32[]{:S(2)}) copy-start(f32[3,256,256]{2,1,0:T(8,128)} %param.17) | copy-start | bytes 2359300
  29.3 19.3 %all-to-all-start.1 = ((f32[32,1,256]{2,1,0:T(1,128)}), f32[32,1,256]{2,1,0:T(1,128)S(1)}, u32[]{:S(2)}, u32[]{:S(2)}) async-start(f32[32,1,256]{2,1,0:T(1,128)} %reduce_sum.116), calls=%async_computation.1 | async-start | bytes 65536 | tf_op jit(solution)/shard_map/all_to_all | solution.py:30
  49.3 12.4 %all-to-all-start.2 = ((f32[32,1,256]{2,1,0:T(1,128)}), f32[32,1,256]{2,1,0:T(1,128)S(1)}, u32[]{:S(2)}, u32[]{:S(2)}) async-start(f32[32,1,256]{2,1,0:T(1,128)} %broadcast_in_dim.66), calls=%async_computation.2 | async-start | bytes 65536 | tf_op jit(solution)/shard_map/all_to_all | solution.py:41
  62.5 14.2 %all-to-all-start.3 = ((f32[8,32,1,256]{3,1,2,0:T(8,128)}), f32[8,32,1,256]{3,1,2,0:T(8,128)S(1)}, u32[]{:S(2)}, u32[]{:S(2)}) async-start(f32[8,32,1,256]{3,1,2,0:T(8,128)} %broadcast_in_dim.68), calls=%async_computation.3 | async-start | bytes 524288 | tf_op jit(solution)/shard_map/all_to_all | solution.py:41
  139.1 6.0 %copy-start.4 = (f32[32,16,8,256]{3,2,1,0:T(8,128)S(1)}, f32[32,16,8,256]{3,2,1,0:T(8,128)}, u32[]{:S(2)}) copy-start(f32[32,16,8,256]{3,2,1,0:T(8,128)} %param.15) | copy-start | bytes 12582916
  187.9 13.4 %all-to-all-start.7 = ((f32[8,32,1,256]{3,1,2,0:T(8,128)}), f32[8,32,1,256]{3,1,2,0:T(8,128)S(1)}, u32[]{:S(2)}, u32[]{:S(2)}) async-start(f32[8,32,1,256]{3,1,2,0:T(8,128)} %broadcast_in_dim.131), calls=%async_computation.7 | async-start | bytes 524288 | tf_op jit(solution)/shard_map/all_to_all | solution.py:41
  265.0 6.1 %copy-start.2 = (f32[4096,256]{1,0:T(8,128)S(1)}, f32[4096,256]{1,0:T(8,128)}, u32[]{:S(2)}) copy-start(f32[4096,256]{1,0:T(8,128)} %get-tuple-element.147) | copy-start | bytes 12582916
  276.2 44.5 %copy-start.11 = (f32[32,16,8]{0,2,1:T(8,128)S(1)}, f32[32,16,8]{0,2,1:T(8,128)}, u32[]{:S(2)}) copy-start(f32[32,16,8]{0,2,1:T(8,128)} %param.24) | copy-start | bytes 49156
  276.2 44.5 %copy-start.12 = (f32[32,16,8]{0,2,1:T(8,128)S(1)}, f32[32,16,8]{0,2,1:T(8,128)}, u32[]{:S(2)}) copy-start(f32[32,16,8]{0,2,1:T(8,128)} %param.23) | copy-start | bytes 49156
  276.2 44.5 %copy-start.13 = (f32[32,16,8]{0,2,1:T(8,128)S(1)}, f32[32,16,8]{0,2,1:T(8,128)}, u32[]{:S(2)}) copy-start(f32[32,16,8]{0,2,1:T(8,128)} %param.22) | copy-start | bytes 49156
  313.9 13.3 %all-to-all-start.11 = ((f32[8,32,1,256]{3,1,2,0:T(8,128)}), f32[8,32,1,256]{3,1,2,0:T(8,128)S(1)}, u32[]{:S(2)}, u32[]{:S(2)}) async-start(f32[8,32,1,256]{3,1,2,0:T(8,128)} %broadcast_in_dim.136), calls=%async_computation.11 | async-start | bytes 524288 | tf_op jit(solution)/shard_map/all_to_all | solution.py:41
  390.7 5.8 %copy-start.3 = (f32[4096,256]{1,0:T(8,128)S(1)}, f32[4096,256]{1,0:T(8,128)}, u32[]{:S(2)}) copy-start(f32[4096,256]{1,0:T(8,128)} %get-tuple-element.151) | copy-start | bytes 12582916
  400.0 14.5 %copy-start = (f32[4096,256]{1,0:T(8,128)}, f32[4096,256]{1,0:T(8,128)S(1)}, u32[]{:S(2)}) copy-start(f32[4096,256]{1,0:T(8,128)S(1)} %convolution_add_fusion) | copy-start | bytes 12582916
  400.0 9.1 %collective-permute-start = (f32[2,16,8,256]{3,2,1,0:T(8,128)S(1)}, f32[2,16,8,256]{3,2,1,0:T(8,128)S(1)}, u32[]{:S(2)}, u32[]{:S(2)}) collective-permute-start(f32[2,16,8,256]{3,2,1,0:T(8,128)S(1)} %bitcast.281), channel_id=1, source_target_pairs={{0,32},{32,64},{64,96},{96,128},{128,160},{160,192},{192,224},{1,3... | collective-permute-start | bytes 786440 | tf_op jit(solution)/shard_map/ppermute | solution.py:71
  402.4 8.4 %collective-permute-start.1 = (f32[2,16,8,256]{3,2,1,0:T(8,128)S(1)}, f32[2,16,8,256]{3,2,1,0:T(8,128)S(1)}, u32[]{:S(2)}, u32[]{:S(2)}) collective-permute-start(f32[2,16,8,256]{3,2,1,0:T(8,128)S(1)} %bitcast.280), channel_id=1, source_target_pairs={{32,0},{64,32},{96,64},{128,96},{160,128},{192,160},{224,192},{33,... | collective-permute-start | bytes 786440 | tf_op jit(solution)/shard_map/ppermute | solution.py:72
  403.8 10.6 %collective-permute-start.4 = (f32[3,1,16,8]{1,3,2,0:T(8,128)S(1)}, f32[3,1,16,8]{1,3,2,0:T(8,128)S(1)}, u32[]{:S(2)}, u32[]{:S(2)}) collective-permute-start(f32[3,1,16,8]{1,3,2,0:T(8,128)S(1)} %get-tuple-element.101), channel_id=1, source_target_pairs={{0,32},{32,64},{64,96},{96,128},{128,160},{160,192},{192,224},{1,3... | collective-permute-start | bytes 4616 | tf_op jit(solution)/shard_map/ppermute | solution.py:71
  407.8 6.6 %collective-permute-start.5 = (f32[3,1,16,8]{1,3,2,0:T(8,128)S(1)}, f32[3,1,16,8]{1,3,2,0:T(8,128)S(1)}, u32[]{:S(2)}, u32[]{:S(2)}) collective-permute-start(f32[3,1,16,8]{1,3,2,0:T(8,128)S(1)} %get-tuple-element.102), channel_id=1, source_target_pairs={{32,0},{64,32},{96,64},{128,96},{160,128},{192,160},{224,192},{33,... | collective-permute-start | bytes 4616 | tf_op jit(solution)/shard_map/ppermute | solution.py:72
  411.9 14.8 %collective-permute-start.2 = (f32[36,2,8,256]{3,2,1,0:T(8,128)}, f32[36,2,8,256]{3,2,1,0:T(8,128)S(1)}, u32[]{:S(2)}, u32[]{:S(2)}) collective-permute-start(f32[36,2,8,256]{3,2,1,0:T(8,128)} %get-tuple-element.90), channel_id=1, source_target_pairs={{0,1},{1,2},{2,3},{3,4},{4,5},{5,6},{6,7},{7,8},{8,9},{9,10},{10,1... | collective-permute-start | bytes 1769480 | tf_op jit(solution)/shard_map/ppermute | solution.py:71
  414.4 12.2 %collective-permute-start.3 = (f32[36,2,8,256]{3,2,1,0:T(8,128)}, f32[36,2,8,256]{3,2,1,0:T(8,128)S(1)}, u32[]{:S(2)}, u32[]{:S(2)}) collective-permute-start(f32[36,2,8,256]{3,2,1,0:T(8,128)} %get-tuple-element.91), channel_id=1, source_target_pairs={{1,0},{2,1},{3,2},{4,3},{5,4},{6,5},{7,6},{8,7},{9,8},{10,9},{11,1... | collective-permute-start | bytes 1769480 | tf_op jit(solution)/shard_map/ppermute | solution.py:72
  414.5 9.5 %collective-permute-start.6 = (f32[3,34,1,8]{1,3,2,0:T(8,128)S(1)}, f32[3,34,1,8]{1,3,2,0:T(8,128)S(1)}, u32[]{:S(2)}, u32[]{:S(2)}) collective-permute-start(f32[3,34,1,8]{1,3,2,0:T(8,128)S(1)} %get-tuple-element.94), channel_id=1, source_target_pairs={{0,1},{1,2},{2,3},{3,4},{4,5},{5,6},{6,7},{7,8},{8,9},{9,10},{10,1... | collective-permute-start | bytes 9800 | tf_op jit(solution)/shard_map/ppermute | solution.py:71
  417.8 6.5 %collective-permute-start.7 = (f32[3,34,1,8]{1,3,2,0:T(8,128)S(1)}, f32[3,34,1,8]{1,3,2,0:T(8,128)S(1)}, u32[]{:S(2)}, u32[]{:S(2)}) collective-permute-start(f32[3,34,1,8]{1,3,2,0:T(8,128)S(1)} %get-tuple-element.95), channel_id=1, source_target_pairs={{1,0},{2,1},{3,2},{4,3},{5,4},{6,5},{7,6},{8,7},{9,8},{10,9},{11,1... | collective-permute-start | bytes 9800 | tf_op jit(solution)/shard_map/ppermute | solution.py:72
  426.6 3.5 copy-start.1
  426.6 3.6 copy-start.5
  430.2 6.4 %copy-start.6 = (f32[32,16,8]{2,1,0:T(8,128)S(1)}, f32[32,16,8]{2,1,0:T(8,128)}, u32[]{:S(2)}) copy-start(f32[32,16,8]{2,1,0:T(8,128)} %copy.110) | copy-start | bytes 49156
  430.2 6.5 %copy-start.7 = (f32[32,16,8]{2,1,0:T(8,128)S(1)}, f32[32,16,8]{2,1,0:T(8,128)}, u32[]{:S(2)}) copy-start(f32[32,16,8]{2,1,0:T(8,128)} %copy.106) | copy-start | bytes 49156
  430.2 6.5 %copy-start.8 = (f32[32,16,8]{2,1,0:T(8,128)S(1)}, f32[32,16,8]{2,1,0:T(8,128)}, u32[]{:S(2)}) copy-start(f32[32,16,8]{2,1,0:T(8,128)} %copy.107) | copy-start | bytes 49156
  430.2 6.5 %copy-start.9 = (f32[32,16,8]{2,1,0:T(8,128)S(1)}, f32[32,16,8]{2,1,0:T(8,128)}, u32[]{:S(2)}) copy-start(f32[32,16,8]{2,1,0:T(8,128)} %copy.108) | copy-start | bytes 49156
  430.2 6.5 %copy-start.10 = (f32[32,16,8]{2,1,0:T(8,128)S(1)}, f32[32,16,8]{2,1,0:T(8,128)}, u32[]{:S(2)}) copy-start(f32[32,16,8]{2,1,0:T(8,128)} %copy.109) | copy-start | bytes 49156
where the time goes:
time: 449 us; the launch traced here: 442 us
  other arithmetic  190 us (42%)
  blocking collectives  66.4 us (15%)
  starting transfers between devices  59 us (13%)
  matrix products  40 us (9%)
  local copies, waits for them, and re-layouts  36.7 us (8%)
  waiting for transfers between devices  36.2 us (8%)
  between operations  14.2 us (3%)
    another operation x20, other arithmetic, analysis(): factor = jnp.linalg.cholesky(covariance)  103 us
    another operation x7, other arithmetic, analysis(): jax.scipy.linalg.solve_triangular(factor, inner, lower=True, trans=1)  59.9 us
    all_to_all x4, waiting for transfers between devices, sent_to_all(): lax.all_to_all(jnp.broadcast_to(x[None], (size, *x.shape)), axis, 0, 0, t...  25.4 us
    all_to_all x4, starting transfers between devices, sent_to_all(): lax.all_to_all(jnp.broadcast_to(x[None], (size, *x.shape)), axis, 0, 0, t...  25.3 us
    all_to_all x2, blocking collectives, sent_to_all(): lax.all_to_all(jnp.broadcast_to(x[None], (size, *x.shape)), axis, 0, 0, t...  23.3 us
    all_to_all x2, blocking collectives, summed_rows(): lax.all_to_all(nearer, far, split_axis=0, concat_axis=0, tiled=True)  23.2 us
    all_to_all x2, blocking collectives, sent_and_summed(): lax.all_to_all(tiles, axis, split_axis=0, concat_axis=0, tiled=True)  19.9 us
    dot_general x3, matrix products, regress(): jnp.dot(anomaly, spread.T, precision=lax.Precision.HIGHEST) / (members - 1)  17.8 us
  transfers between devices with their start and end apart: 14, of which 7 were waited for; matrix products, arithmetic and copies ran while one was open for 4% of the time, Pallas kernels for 0%

commit v1 on v0

v1 whole, which is shorter than its diff:
```python
import functools

import jax
import jax.numpy as jnp
from jax import lax
from jax.experimental import pallas as pl
from jax.experimental.pallas import tpu as pltpu
from jax.sharding import PartitionSpec as P

F32 = jnp.float32
BF16 = jnp.bfloat16
HI = lax.Precision.HIGHEST
MESH = pl.DeviceIdType.MESH
NN = (((1,), (0,)), ((), ()))
NT = (((1,), (1,)), ((), ()))
TN = (((0,), (0,)), ((), ()))

LEV = 8
NB = 3
CLAT = 32
CLON = 16
NOBS = 256
MEM = 256
PIV = 4
PANEL = 32
VM = pltpu.VMEM
SM = pltpu.SMEM


def pick_kernel(cells_ref, own_ref, state_ref, out_ref):
    for b in range(NB):
        own = own_ref[b]

        def body(o, carry):
            for u in range(8):
                c = cells_ref[b, o * 8 + u]
                out_ref[b, pl.ds(o * 8 + u, 1), :] = state_ref[pl.ds(c, 1), :] * own
            return carry

        lax.fori_loop(0, NOBS // 8, body, 0)


def exchange_kernel(
    nlat,
    nlon,
    picked,
    edges,
    ens,
    rows,
    edges_in,
    ext,
    got1,
    got2,
    part1,
    part2,
    s1,
    r1,
    s2,
    r2,
    s3,
    r3,
    hs,
    hr,
    es,
    er,
    loc,
):
    l = lax.axis_index("lat")
    n = lax.axis_index("lon")
    piece = NOBS // nlon
    lm, lp = lax.rem(l + nlat - 1, nlat), lax.rem(l + 1, nlat)
    nm, np_ = lax.rem(n + nlon - 1, nlon), lax.rem(n + 1, nlon)

    bar = pltpu.get_barrier_semaphore()

    def greet_lon(r, carry):
        pl.semaphore_signal(bar, inc=1, device_id=(l, lax.rem(n + r, nlon)), device_id_type=MESH)
        return carry

    def greet_lat(r, carry):
        pl.semaphore_signal(bar, inc=1, device_id=(lax.rem(l + r, nlat), n), device_id_type=MESH)
        return carry

    lax.fori_loop(1, nlon, greet_lon, 0)
    lax.fori_loop(1, nlat, greet_lat, 0)
    for a in (lm, lp):
        for c in (nm, np_):
            pl.semaphore_signal(bar, inc=1, device_id=(a, c), device_id_type=MESH)
    pl.semaphore_wait(bar, nlon - 1 + nlat - 1 + 4)

    local = pltpu.make_async_copy(ens, ext.at[pl.ds(2, CLAT), pl.ds(2, CLON)], loc)
    local.start()

    groups = ((0, 1), (1, 2))

    def send1(g):
        b0, nb = groups[g]

        def go(r, carry):
            peer = lax.rem(n + r, nlon)
            pltpu.make_async_remote_copy(
                src_ref=picked.at[pl.ds(b0, nb), pl.ds(peer * piece, piece)],
                dst_ref=got1.at[r - 1, pl.ds(b0, nb)],
                send_sem=s1.at[g],
                recv_sem=r1.at[g],
                device_id=(l, peer),
                device_id_type=MESH,
            ).start()
            return carry

        lax.fori_loop(1, nlon, go, 0)

    def wait1(g):
        b0, nb = groups[g]
        full = got1.at[:, pl.ds(b0, nb)]
        pltpu.make_async_copy(full, full, r1.at[g]).wait()

    def send2(g):
        b0, nb = groups[g]
        tot = picked[pl.ds(b0, nb), pl.ds(pl.multiple_of(n * piece, piece), piece), :]
        for i in range(nlon - 1):
            tot = tot + got1[i, pl.ds(b0, nb)]
        part1[pl.ds(b0, nb)] = tot

        def go(r, carry):
            peer = lax.rem(l + r, nlat)
            pltpu.make_async_remote_copy(
                src_ref=part1.at[pl.ds(b0, nb)],
                dst_ref=got2.at[r - 1, pl.ds(b0, nb)],
                send_sem=s2.at[g],
                recv_sem=r2.at[g],
                device_id=(peer, n),
                device_id_type=MESH,
            ).start()
            return carry

        lax.fori_loop(1, nlat, go, 0)

    def wait2(g):
        b0, nb = groups[g]
        full = got2.at[:, pl.ds(b0, nb)]
        pltpu.make_async_copy(full, full, r2.at[g]).wait()

    def send3(g):
        b0, nb = groups[g]
        tot = part1[pl.ds(b0, nb)]
        for i in range(nlat - 1):
            tot = tot + got2[i, pl.ds(b0, nb)]
        part2[pl.ds(b0, nb)] = tot
        mine = pl.ds(pl.multiple_of(n * piece, piece), piece)
        rows[pl.ds(b0, nb), mine, :] = tot

        def go(r, carry):
            peer = lax.rem(n + r, nlon)
            pltpu.make_async_remote_copy(
                src_ref=part2.at[pl.ds(b0, nb)],
                dst_ref=rows.at[pl.ds(b0, nb), mine],
                send_sem=s3.at[g],
                recv_sem=r3.at[g],
                device_id=(l, peer),
                device_id_type=MESH,
            ).start()
            return carry

        lax.fori_loop(1, nlon, go, 0)

    def wait3(g):
        b0, nb = groups[g]
        full = rows.at[pl.ds(b0, nb), pl.ds(0, NOBS - piece)]
        pltpu.make_async_copy(full, full, r3.at[g]).wait()

    send1(0)
    send1(1)
    wait1(0)
    send2(0)
    wait2(0)
    send3(0)
    wait1(1)
    send2(1)
    wait2(1)
    send3(1)

    moves = (
        ((lm, n), (0, 2, 0, CLON), (34, 2)),
        ((lp, n), (CLAT - 2, 2, 0, CLON), (0, 2)),
        ((l, nm), (0, CLAT, 0, 2), (2, 18)),
        ((l, np_), (0, CLAT, CLON - 2, 2), (2, 0)),
        ((lm, nm), (0, 1, 0, 1), (34, 18)),
        ((lm, np_), (0, 1, CLON - 1, 1), (34, 1)),
        ((lp, nm), (CLAT - 1, 1, 0, 1), (1, 18)),
        ((lp, np_), (CLAT - 1, 1, CLON - 1, 1), (1, 1)),
    )
    copies = []
    for i, (dev, (i0, ni, j0, nj), (di, dj)) in enumerate(moves):
        copies.append(
            pltpu.make_async_remote_copy(
                src_ref=ens.at[pl.ds(i0, ni), pl.ds(j0, nj)],
                dst_ref=ext.at[pl.ds(di, ni), pl.ds(dj, nj)],
                send_sem=hs.at[i],
                recv_sem=hr.at[i],
                device_id=dev,
                device_id_type=MESH,
            )
        )
        if i < 4:
            copies.append(
                pltpu.make_async_remote_copy(
                    src_ref=edges.at[i],
                    dst_ref=edges_in.at[i],
                    send_sem=es.at[i],
                    recv_sem=er.at[i],
                    device_id=dev,
                    device_id_type=MESH,
                )
            )
    for c in copies:
        c.start()
    wait3(0)
    wait3(1)
    for g in range(2):
        b0, nb = groups[g]
        src = picked.at[pl.ds(b0, nb), pl.ds(0, NOBS - piece)]
        pltpu.make_async_copy(src, src, s1.at[g]).wait()
        full = got2.at[:, pl.ds(b0, nb)]
        pltpu.make_async_copy(full, full, s2.at[g]).wait()
        pltpu.make_async_copy(src, src, s3.at[g]).wait()
    for c in copies:
        c.wait()
    local.wait()


def ssum(xs):
    xs = list(xs)
    while len(xs) > 1:
        xs = [xs[i] + xs[i + 1] if i + 1 < len(xs) else xs[i] for i in range(0, len(xs), 2)]
    return xs[0]


def inv_sym(p, b):
    if b == 1:
        return {(0, 0): 1.0 / p[0, 0]}
    if b == 2:
        a, c, d = p[0, 0], p[0, 1], p[1, 1]
        r = 1.0 / (a * d - c * c)
        off = -(c * r)
        return {(0, 0): d * r, (0, 1): off, (1, 0): off, (1, 1): a * r}
    h = b // 2
    hs = range(h)
    A = inv_sym({(s, t): p[s, t] for s in hs for t in range(s, h)}, h)
    B = {(s, t): p[s, h + t] for s in hs for t in hs}
    AB = {(s, t): ssum(A[s, u] * B[u, t] for u in hs) for s in hs for t in hs}
    S = {
        (s, t): p[h + s, h + t] - ssum(B[u, s] * AB[u, t] for u in hs)
        for s in hs
        for t in range(s, h)
    }
    Si = inv_sym(S, h)
    ABS = {(s, t): ssum(AB[s, u] * Si[u, t] for u in hs) for s in hs for t in hs}
    Q = {}
    for s in hs:
        for t in hs:
            Q[s, t] = A[s, t] + ssum(ABS[s, u] * AB[t, u] for u in hs)
            Q[s, h + t] = -ABS[s, t]
            Q[h + t, s] = Q[s, h + t]
            Q[h + s, h + t] = Si[s, t]
    return Q


def sweep_slab(tiles, base, b, nrow):
    rt_n, lt_n = nrow // 8, len(tiles[0])
    lane = lax.broadcasted_iota(jnp.int32, (8, 128), 1)
    sub = lax.broadcasted_iota(jnp.int32, (8, 128), 0)
    tiles = [list(r) for r in tiles]
    full = (8, 128)
    for c in range(0, nrow, b):
        ltc, l0 = (base + c) // 128, (base + c) % 128
        rt0, s0 = c // 8, c % 8
        rows = [
            [jnp.broadcast_to(tiles[rt0][lt][s0 + s : s0 + s + 1, :], full) for lt in range(lt_n)]
            for s in range(b)
        ]
        cols = [
            [
                jnp.broadcast_to(tiles[rt][ltc][:, l0 + s : l0 + s + 1], full)
                for rt in range(rt_n)
            ]
            for s in range(b)
        ]
        p = {
            (s, t): jnp.broadcast_to(rows[s][ltc][:, l0 + t : l0 + t + 1], full)
            for s in range(b)
            for t in range(s, b)
        }
        Q = inv_sym(p, b)
        colm = jnp.logical_and(lane >= l0, lane < l0 + b)
        R = []
        for s in range(b):
            rr = []
            for lt in range(lt_n):
                acc = ssum(Q[s, t] * rows[t][lt] for t in range(b))
                if lt == ltc:
                    for t in range(b):
                        acc = jnp.where(lane == l0 + t, -Q[s, t], acc)
                rr.append(acc)
            R.append(rr)
        for rt in range(rt_n):
            for lt in range(lt_n):
                m = tiles[rt][lt]
                if lt == ltc:
                    m = jnp.where(colm, 0.0, m)
                m = m - ssum(cols[s][rt] * R[s][lt] for s in range(b))
                if rt == rt0:
                    for s in range(b):
                        m = jnp.where(sub == s0 + s, R[s][lt], m)
                tiles[rt][lt] = m
    return tiles


def split3(x):
    h = x.astype(BF16)
    r = x - h.astype(F32)
    m = r.astype(BF16)
    return h, m, (r - m.astype(F32)).astype(BF16)


def split2(x):
    h = x.astype(BF16)
    return h, (x - h.astype(F32)).astype(BF16)


def eliminate(m_ref):
    nb = PANEL
    lane = lax.broadcasted_iota(jnp.int32, (nb, 256), 1)
    cm = lax.broadcasted_iota(jnp.int32, (1, 128), 1)
    count = 256 // nb
    for k in range(count):
        r0 = k * nb
        slab = m_ref[r0 : r0 + nb, 0:256]
        tiles = [
            [m_ref[r0 + 8 * rt : r0 + 8 * rt + 8, 128 * lt : 128 * lt + 128] for lt in range(4)]
            for rt in range(nb // 8)
        ]
        tiles = sweep_slab(tiles, r0, PIV, nb)
        R = jnp.concatenate([jnp.concatenate(t, axis=1) for t in tiles], axis=0)
        left = jnp.where(jnp.logical_and(lane >= r0, lane < r0 + nb), 0.0, slab)
        lh, lm, ll = split3(left)
        rh, rm, rl = split3(R)
        la = jnp.concatenate([lh, lh, lm, lh, lm, ll], axis=0)
        ra = jnp.concatenate([rh, rm, rh, rl, rm, rh], axis=0)
        l0 = (r0 // 128) * 128
        here = jnp.logical_and(cm >= r0 - l0, cm < r0 - l0 + nb)

        def apply(a, z):
            u = lax.dot_general(la[:, a:z], ra, TN, preferred_element_type=F32)
            for lt in range(4):
                cur = m_ref[a:z, 128 * lt : 128 * lt + 128]
                if 128 * lt == l0:
                    cur = jnp.where(here, 0.0, cur)
                m_ref[a:z, 128 * lt : 128 * lt + 128] = cur - u[:, 128 * lt : 128 * lt + 128]

        if k + 1 < count:
            apply(r0 + nb, r0 + 2 * nb)
            if r0 > 0:
                apply(0, r0)
            if r0 + 2 * nb < 256:
                apply(r0 + 2 * nb, 256)
        else:
            apply(0, r0)
        m_ref[r0 : r0 + nb, :] = R


def main_kernel(
    nlat,
    nlon,
    place,
    tiles_ref,
    radius_ref,
    rows_in,
    noise_ref,
    values_ref,
    var_ref,
    cells_ref,
    alat,
    alon,
    diff,
    edge_ref,
    ext,
    out,
    rows_ref,
    x_ref,
    mid_ref,
    o_ref,
    cb_ref,
    m_ref,
    sth_ref,
    stl_ref,
    wh_ref,
    wm_ref,
    wl_ref,
    u_ref,
    v_ref,
    insem,
    outsem,
):
    l = place[0]
    n = place[1]
    load = pltpu.make_async_copy(ext, x_ref, insem)
    load.start()
    for b in range(NB):
        rows_ref[b] = rows_in[b]

    def derived(a, e, k):
        return (
            1.0 - jnp.abs(a) - jnp.abs(e) - 4.0 * k,
            jnp.maximum(a, 0.0) + k,
            k - jnp.minimum(a, 0.0),
            jnp.maximum(e, 0.0) + k,
            k - jnp.minimum(e, 0.0),
        )

    def inner(q, carry):
        i0 = q * 8
        cells = [
            jnp.transpose(r[pl.ds(i0, 8)].reshape(128, LEV)) for r in (alat, alon, diff)
        ]
        for f, d in enumerate(derived(*cells)):
            for i in range(8):
                for j in range(CLON):
                    t = i * CLON + j
                    cb_ref[f, i0 + 1 + i, 1 + j] = jnp.broadcast_to(d[:, t : t + 1], (8, 128))
        return carry

    lax.fori_loop(0, CLAT // 8, inner, 0)
    for d in range(4):
        der = derived(edge_ref[d, 0], edge_ref[d, 1], edge_ref[d, 2])
        if d < 2:
            outside = (l == nlat - 1) if d == 0 else (l == 0)
            keep = jnp.where(outside, 0.0, 1.0)
        for f in range(5):
            w = der[f] * keep if d < 2 else der[f]
            for t in range(CLON if d < 2 else CLAT):
                spread = jnp.broadcast_to(w[:, t : t + 1], (8, 128))
                if d == 0:
                    cb_ref[f, CLAT + 1, 1 + t] = spread
                elif d == 1:
                    cb_ref[f, 0, 1 + t] = spread
                elif d == 2:
                    cb_ref[f, 1 + t, CLON + 1] = spread
                else:
                    cb_ref[f, 1 + t, 0] = spread

    ri = lax.broadcasted_iota(jnp.int32, (256, 256), 0)
    ci = lax.broadcasted_iota(jnp.int32, (256, 256), 1)
    eye = ri == ci
    total_lon = float(CLON * nlon)

    def column(row):
        return jnp.sum(jnp.where(eye, row, 0.0), axis=1, keepdims=True)

    def where_obs(b):
        pos = lax.shift_right_logical(cells_ref[pl.ds(b, 1), :], 3)
        lat = tiles_ref[b, 0] * CLAT + lax.shift_right_logical(pos, 4)
        lon = tiles_ref[b, 1] * CLON + jnp.bitwise_and(pos, 15)
        return lat.astype(F32), lon.astype(F32)

    def lon_sq(gap):
        gap = jnp.abs(gap)
        gap = jnp.minimum(gap, total_lon - gap)
        return gap * gap

    load.wait()

    def batch(b, carry):
        rows = rows_ref[b]
        spread = rows - jnp.mean(rows, axis=1, keepdims=True)
        var = var_ref[pl.ds(b, 1), :]
        cov = lax.dot_general(spread, spread, NT, precision=HI, preferred_element_type=F32)
        m_ref[:, 0:256] = cov * (1.0 / (MEM - 1)) + jnp.where(eye, var, 0.0)
        m_ref[:, 256:512] = (
            column(values_ref[pl.ds(b, 1), :])
            + column(jnp.sqrt(var)) * noise_ref[b]
            - rows
        )
        spread_t = jnp.transpose(spread) * (1.0 / (MEM - 1))
        hi, lo = split2(spread_t)
        sth_ref[...] = hi
        stl_ref[...] = lo
        eliminate(m_ref)
        weights = m_ref[:, 256:512]
        wh_ref[...], wm_ref[...], wl_ref[...] = split3(weights)

        reach = radius_ref[b].astype(F32)
        inv_sq = 1.0 / (jnp.full((1, 256), 1.0, F32) * (reach * reach))
        obs_lat, obs_lon = where_obs(b)

        def later(c, carry):
            r = rows_ref[c]
            mine_lat, mine_lon = where_obs(c)
            dlat = column(mine_lat) - obs_lat
            d2 = dlat * dlat + lon_sq(column(mine_lon) - obs_lon)
            taper = jnp.maximum(1.0 - d2 * inv_sq, 0.0)
            an = r - jnp.mean(r, axis=1, keepdims=True)
            reg = lax.dot_general(an, spread_t, NN, precision=HI, preferred_element_type=F32)
            reg = reg * (taper * taper)
            rows_ref[c] = r + lax.dot_general(
                reg, weights, NN, precision=HI, preferred_element_type=F32
            )
            return carry

        lax.fori_loop(b + 1, NB, later, 0)

        for j in range(CLON + 4):
            pos = lax.rem(n * CLON + j - 2 + CLON * nlon, CLON * nlon).astype(F32)
            v_ref[j] = jnp.broadcast_to(lon_sq(pos - obs_lon) * inv_sq, (8, 256))

        def lat_row(i, carry):
            gap = (l * CLAT + i - 2).astype(F32) - obs_lat
            u_ref[i] = jnp.broadcast_to(1.0 - gap * gap * inv_sq, (8, 256))
            return carry

        lax.fori_loop(0, CLAT + 4, lat_row, 0)

        def block(i, carry):
            x = x_ref[pl.ds(4 * i, 4)].reshape(4 * 20 * 8, 256)
            an = x - jnp.mean(x, axis=1, keepdims=True)
            ah, al = split2(an)
            sh, sl = sth_ref[...], stl_ref[...]
            dot = functools.partial(lax.dot_general, dimension_numbers=NN, preferred_element_type=F32)
            reg = dot(ah, sh) + dot(al, sh) + dot(ah, sl)
            tap = jnp.maximum(u_ref[pl.ds(4 * i, 4)][:, None] - v_ref[...][None], 0.0)
            reg = reg * (tap * tap).reshape(4 * 20 * 8, 256)
            gh, gm, gl = split3(reg)
            wh, wm, wl = wh_ref[...], wm_ref[...], wl_ref[...]
            small = dot(gm, wm) + dot(gh, wl) + dot(gl, wh)
            x = x + (dot(gh, wh) + ((dot(gm, wh) + dot(gh, wm)) + small))
            x_ref[pl.ds(4 * i, 4)] = x.reshape(4, 20, 8, 256)
            return carry

        lax.fori_loop(0, 9, block, 0)
        return carry

    lax.fori_loop(0, NB, batch, 0)

    @pl.when(l == 0)
    def _():
        x_ref[0:2] = jnp.zeros((2, CLON + 4, LEV, MEM), F32)

    @pl.when(l == nlat - 1)
    def _():
        x_ref[CLAT + 2 : CLAT + 4] = jnp.zeros((2, CLON + 4, LEV, MEM), F32)

    def first(i, carry):
        for h in range(2):
            m = pl.ds(128 * h, 128)
            mid_ref[i, :, :, m] = (
                cb_ref[0, i] * x_ref[i + 1, 1:19, :, m]
                + cb_ref[1, i] * x_ref[i, 1:19, :, m]
                + cb_ref[2, i] * x_ref[i + 2, 1:19, :, m]
                + cb_ref[3, i] * x_ref[i + 1, 0:18, :, m]
                + cb_ref[4, i] * x_ref[i + 1, 2:20, :, m]
            )
        return carry

    lax.fori_loop(0, CLAT + 2, first, 0)

    def second(i, carry):
        for h in range(2):
            m = pl.ds(128 * h, 128)
            o_ref[i, :, :, m] = (
                cb_ref[0, i + 1, 1:17] * mid_ref[i + 1, 1:17, :, m]
                + cb_ref[1, i + 1, 1:17] * mid_ref[i, 1:17, :, m]
                + cb_ref[2, i + 1, 1:17] * mid_ref[i + 2, 1:17, :, m]
                + cb_ref[3, i + 1, 1:17] * mid_ref[i + 1, 0:16, :, m]
                + cb_ref[4, i + 1, 1:17] * mid_ref[i + 1, 2:18, :, m]
            )
        pltpu.make_async_copy(o_ref.at[i], out.at[i], outsem).start()
        return carry

    lax.fori_loop(0, CLAT, second, 0)
    pltpu.make_async_copy(o_ref, out, outsem).wait()


def shards(
    nlat,
    nlon,
    ensemble,
    obs_values,
    obs_noise,
    obs_var,
    obs_cells,
    owner_tiles,
    radius,
    courant_lat,
    courant_lon,
    diffusivity,
):
    l = lax.axis_index("lat")
    n = lax.axis_index("lon")
    own = jnp.logical_and(owner_tiles[:, 0] == l, owner_tiles[:, 1] == n).astype(F32)
    place = jnp.stack([l, n]).astype(jnp.int32)

    picked = pl.pallas_call(
        pick_kernel,
        out_shape=jax.ShapeDtypeStruct((NB, NOBS, MEM), F32),
        in_specs=[
            pl.BlockSpec(memory_space=SM),
            pl.BlockSpec(memory_space=SM),
            pl.BlockSpec(memory_space=VM),
        ],
        out_specs=pl.BlockSpec(memory_space=VM),
        compiler_params=pltpu.CompilerParams(vmem_limit_bytes=24 << 20),
        name="pick",
    )(obs_cells, own, ensemble.reshape(-1, MEM))

    coefs = jnp.stack([courant_lat, courant_lon, diffusivity])
    pad = lambda x: jnp.pad(x, ((0, 0), (0, 0), (0, 32 - x.shape[2])))
    edges = jnp.stack(
        [
            pad(jnp.swapaxes(coefs[:, 0], 1, 2)),
            pad(jnp.swapaxes(coefs[:, CLAT - 1], 1, 2)),
            jnp.swapaxes(coefs[:, :, 0], 1, 2),
            jnp.swapaxes(coefs[:, :, CLON - 1], 1, 2),
        ]
    )
    piece = NOBS // nlon
    dma = pltpu.SemaphoreType.DMA
    rows, edges_in, ext = pl.pallas_call(
        functools.partial(exchange_kernel, nlat, nlon),
        out_shape=(
            jax.ShapeDtypeStruct((NB, NOBS, MEM), F32),
            jax.ShapeDtypeStruct((4, 3, LEV, 32), F32),
            jax.ShapeDtypeStruct((CLAT + 4, CLON + 4, LEV, MEM), F32),
        ),
        in_specs=[
            pl.BlockSpec(memory_space=VM),
            pl.BlockSpec(memory_space=VM),
            pl.BlockSpec(memory_space=pl.ANY),
        ],
        out_specs=(
            pl.BlockSpec(memory_space=VM),
            pl.BlockSpec(memory_space=VM),
            pl.BlockSpec(memory_space=pl.ANY),
        ),
        scratch_shapes=[
            pltpu.VMEM((nlon - 1, NB, piece, MEM), F32),
            pltpu.VMEM((nlat - 1, NB, piece, MEM), F32),
            pltpu.VMEM((NB, piece, MEM), F32),
            pltpu.VMEM((NB, piece, MEM), F32),
            dma((2,)),
            dma((2,)),
            dma((2,)),
            dma((2,)),
            dma((2,)),
            dma((2,)),
            dma((8,)),
            dma((8,)),
            dma((4,)),
            dma((4,)),
            dma,
        ],
        compiler_params=pltpu.CompilerParams(
            collective_id=0, has_side_effects=True, vmem_limit_bytes=56 << 20
        ),
        name="exchange",
    )(picked, edges, ensemble)

    return pl.pallas_call(
        functools.partial(main_kernel, nlat, nlon),
        out_shape=jax.ShapeDtypeStruct((CLAT, CLON, LEV, MEM), F32),
        in_specs=[pl.BlockSpec(memory_space=SM)] * 3
        + [pl.BlockSpec(memory_space=VM)] * 9
        + [pl.BlockSpec(memory_space=pl.ANY)],
        out_specs=pl.BlockSpec(memory_space=pl.ANY),
        scratch_shapes=[
            pltpu.VMEM((NB, NOBS, MEM), F32),
            pltpu.VMEM((CLAT + 4, CLON + 4, LEV, MEM), F32),
            pltpu.VMEM((CLAT + 2, CLON + 2, LEV, MEM), F32),
            pltpu.VMEM((CLAT, CLON, LEV, MEM), F32),
            pltpu.VMEM((5, CLAT + 2, CLON + 2, LEV, 128), F32),
            pltpu.VMEM((256, 512), F32),
            pltpu.VMEM((256, 256), BF16),
            pltpu.VMEM((256, 256), BF16),
            pltpu.VMEM((256, 256), BF16),
            pltpu.VMEM((256, 256), BF16),
            pltpu.VMEM((256, 256), BF16),
            pltpu.VMEM((CLAT + 4, LEV, 256), F32),
            pltpu.VMEM((CLON + 4, LEV, 256), F32),
            dma,
            dma,
        ],
        compiler_params=pltpu.CompilerParams(vmem_limit_bytes=56 << 20),
        name="assimilate",
    )(
        place,
        owner_tiles,
        radius,
        rows,
        obs_noise,
        obs_values,
        obs_var,
        obs_cells,
        courant_lat,
        courant_lon,
        diffusivity,
        edges_in,
        ext,
    )


def solution(mesh):
    nlat, nlon = mesh.shape["lat"], mesh.shape["lon"]
    tile = P("lat", "lon", None)
    return jax.shard_map(
        functools.partial(shards, nlat, nlon),
        mesh=mesh,
        in_specs=(P("lat", "lon", None, None),) + (P(),) * 6 + (tile,) * 3,
        out_specs=P("lat", "lon", None, None),
        check_vma=False,
    )
```

time: 449 us -> 261 us (0.58); the launches traced: 442 us -> 260 us
  Pallas kernels: 0 us -> 246 us
  other arithmetic: 190 us -> 3.67 us
  blocking collectives: 66.4 us -> 0 us
  starting transfers between devices: 59 us -> 0 us
  matrix products: 40 us -> 0 us
  waiting for transfers between devices: 36.2 us -> 0 us
  local copies, waits for them, and re-layouts: 36.7 us -> 10.7 us
  between operations: 14.2 us -> 0.21 us
    pallas_call x0 -> x3, Pallas kernels: none -> 246 us  [the longest x1 139 us: shards(): pl.pallas_call(functools.partial(exchange_kernel, nlat, nlon), out_shape=...]
    another operation x28 -> x4, other arithmetic: 163 us -> 2.91 us  [the longest x2 1.41 us: shards(): jnp.stack([pad(jnp.swapaxes(coefs[:, 0], 1, 2)), pad(jnp.swapaxes(coefs[:...]
    all_to_all x6 -> x0, blocking collectives: 66.4 us -> none  [the longest x2 23.3 us: sent_to_all(): lax.all_to_all(jnp.broadcast_to(x[None], (size, *x.shape)), axis, 0, 0, t...]
    all_to_all x6 -> x0, starting transfers between devices: 42.3 us -> none  [the longest x4 25.3 us: sent_to_all(): lax.all_to_all(jnp.broadcast_to(x[None], (size, *x.shape)), axis, 0, 0, t...]
    all_to_all x6 -> x0, waiting for transfers between devices: 34.2 us -> none  [the longest x4 25.4 us: sent_to_all(): lax.all_to_all(jnp.broadcast_to(x[None], (size, *x.shape)), axis, 0, 0, t...]
    dot_general x9 -> x0, matrix products: 33.5 us -> none  [the longest x3 17.8 us: regress(): jnp.dot(anomaly, spread.T, precision=lax.Precision.HIGHEST) / (members - 1)]
    ppermute x8 -> x0, starting transfers between devices: 16.8 us -> none  [the longest x4 12.2 us: extended(): before = lax.ppermute(last, axis, up)]
    add x7 -> x0, other arithmetic: 11.9 us -> none  [the longest x2 11.8 us: advance(): centre - transport]
  transfers between devices with their start and end apart: 14 -> 0, of which waited for: 7 -> 0; matrix products, arithmetic and copies ran while one was open for 4% -> 0% of each run, Pallas kernels for 0% -> 0%
where the time goes in v1:
time: 261 us; the launch traced here: 260 us
  Pallas kernels  246 us (94%)
  local copies, waits for them, and re-layouts  10.7 us (4%)
  other arithmetic  3.67 us (1%)
    pallas_call x1, Pallas kernels, shards(): pl.pallas_call(functools.partial(exchange_kernel, nlat, nlon), out_shape=...  139 us
    pallas_call x1, Pallas kernels, shards(): pl.pallas_call(functools.partial(main_kernel, nlat, nlon), out_shape=jax....  103 us
    unnamed x10, local copies, waits for them, and re-layouts  10.2 us

profile of v1, /device:TPU:1, one launch (start us, length us, event | category | flops | bytes accessed | tf_op | source)
XLA Modules:
  0.0 260.5 jit_solution(9421661402850612111)
XLA Ops:
  0.0 0.8 fusion.own_ref
  0.8 0.6 pad_add_fusion.place
  1.3 1.3 copy.19.tiles_ref
  2.7 0.8 maximum_bitcast_fusion.1
  3.4 0.9 pad_maximum_fusion
  4.4 0.1 fusion.1
  4.5 0.2 copy.17
  4.7 0.2 copy.18
  4.9 0.6 pad_maximum_fusion.1.edges
  5.6 1.7 copy.20.alat
  7.3 1.7 copy.21.alon
  9.0 1.7 copy.22.diff
  10.7 0.0 copy-start
  10.7 2.2 copy-done
  12.8 0.0 copy-start.2
  12.8 0.7 copy-done.2
  13.5 4.4 %pick.1.picked = f32[3,256,256]{2,1,0:T(8,128)S(1)} custom-call(s32[3,256]{1,0:T(4,128)S(1)} %copy-done.2, f32[3]{0:T(128)S(1)} %fusion.own_ref, f32[4096,256]{1,0:T(8,128)S(1)} %bitcast.30), custom_call_target="tpu_custom_call" | custom-call | tf_op jit(solution)/shard_map/pick/pallas_call | solution.py:602
  17.9 0.0 copy-start.1
  17.9 0.9 copy-done.1
  18.8 138.9 %exchange.1 = (f32[3,256,256]{2,1,0:T(8,128)}, f32[4,3,8,32]{3,2,1,0:T(8,128)}, f32[36,20,8,256]{3,2,1,0:T(8,128)}) custom-call(f32[3,256,256]{2,1,0:T(8,128)} %copy-done.1, f32[4,3,8,32]{3,2,1,0:T(8,128)} %pad_maximum_fusion.1.edges, f32[32,16,8,256]{3,2,1,0:T(8,128)} %ens.1), custom_call_target="tpu_custom_call" | custom-call | tf_op jit(solution)/shard_map/exchange/pallas_call | solution.py:627
  157.7 102.6 %assimilate.1 = f32[32,16,8,256]{3,2,1,0:T(8,128)} custom-call(s32[2]{0:T(128)} %pad_add_fusion.place, s32[3,2]{1,0:T(4,128)} %copy.19.tiles_ref, s32[3]{0:T(128)} %radius_ref.1, f32[3,256,256]{2,1,0:T(8,128)} %get-tuple-element.8.rows_in, f32[3,256,256]{2,1,0:T(8,128)} %noise_ref.1, f32[3,256]{1,0:T(4,128)} %values_ref.1, f32[3,256]{1,0:T(4,128)} %var_ref.1, ...), custom_call_target="tpu_custom_call" | custom-call | tf_op jit(solution)/shard_map/assimilate/pallas_call | solution.py:667
  (1 shorter events, 0.0 us)
Async XLA Ops:
  10.7 2.2 copy-start
  12.8 0.7 copy-start.2
  17.9 0.9 copy-start.1

commit v2 on v1

--- a/solution.py
+++ b/solution.py
@@ -27,28 +27,22 @@
 SM = pltpu.SMEM
 
 
-def pick_kernel(cells_ref, own_ref, state_ref, out_ref):
-    for b in range(NB):
-        own = own_ref[b]
-
-        def body(o, carry):
-            for u in range(8):
-                c = cells_ref[b, o * 8 + u]
-                out_ref[b, pl.ds(o * 8 + u, 1), :] = state_ref[pl.ds(c, 1), :] * own
-            return carry
-
-        lax.fori_loop(0, NOBS // 8, body, 0)
-
-
 def exchange_kernel(
     nlat,
     nlon,
+    tiles_ref,
+    cells_ref,
+    ens,
+    alat,
+    alon,
+    diff,
+    rows,
+    edges_in,
+    place,
+    ext,
+    state,
     picked,
     edges,
-    ens,
-    rows,
-    edges_in,
-    ext,
     got1,
     got2,
     part1,
@@ -71,6 +65,8 @@
     lm, lp = lax.rem(l + nlat - 1, nlat), lax.rem(l + 1, nlat)
     nm, np_ = lax.rem(n + nlon - 1, nlon), lax.rem(n + 1, nlon)
 
+    load = pltpu.make_async_copy(ens, state, loc)
+    load.start()
     bar = pltpu.get_barrier_semaphore()
 
     def greet_lon(r, carry):
@@ -88,8 +84,31 @@
             pl.semaphore_signal(bar, inc=1, device_id=(a, c), device_id_type=MESH)
     pl.semaphore_wait(bar, nlon - 1 + nlat - 1 + 4)
 
-    local = pltpu.make_async_copy(ens, ext.at[pl.ds(2, CLAT), pl.ds(2, CLON)], loc)
-    local.start()
+    place[0] = l
+    place[1] = n
+    lane = lax.broadcasted_iota(jnp.int32, (LEV, 32), 1)
+    for q, coef in enumerate((alat, alon, diff)):
+        edges[2, q] = coef[0]
+        edges[3, q] = coef[CLON - 1]
+        for d, t in ((0, 0), (1, CLAT - 1)):
+            line = jnp.zeros((LEV, 32), F32)
+            for j in range(CLON):
+                line = jnp.where(lane == j, coef[j, :, t : t + 1], line)
+            edges[d, q] = line
+    flat = state.reshape(CLAT * CLON * LEV, MEM)
+
+    def pick(b):
+        own = jnp.logical_and(tiles_ref[0, b] == l, tiles_ref[1, b] == n).astype(F32)
+
+        def body(o, carry):
+            for u in range(8):
+                c = cells_ref[b, o * 8 + u]
+                picked[b, pl.ds(o * 8 + u, 1), :] = flat[pl.ds(c, 1), :] * own
+            return carry
+
+        lax.fori_loop(0, NOBS // 8, body, 0)
+
+    load.wait()
 
     groups = ((0, 1), (1, 2))
 
@@ -169,7 +188,10 @@
         full = rows.at[pl.ds(b0, nb), pl.ds(0, NOBS - piece)]
         pltpu.make_async_copy(full, full, r3.at[g]).wait()
 
+    pick(0)
     send1(0)
+    pick(1)
+    pick(2)
     send1(1)
     wait1(0)
     send2(0)
@@ -226,7 +248,6 @@
         pltpu.make_async_copy(src, src, s3.at[g]).wait()
     for c in copies:
         c.wait()
-    local.wait()
 
 
 def ssum(xs):
@@ -328,45 +349,46 @@
     return h, (x - h.astype(F32)).astype(BF16)
 
 
-def eliminate(m_ref):
+def panel(m_ref, k):
     nb = PANEL
     lane = lax.broadcasted_iota(jnp.int32, (nb, 256), 1)
     cm = lax.broadcasted_iota(jnp.int32, (1, 128), 1)
-    count = 256 // nb
-    for k in range(count):
-        r0 = k * nb
-        slab = m_ref[r0 : r0 + nb, 0:256]
-        tiles = [
-            [m_ref[r0 + 8 * rt : r0 + 8 * rt + 8, 128 * lt : 128 * lt + 128] for lt in range(4)]
-            for rt in range(nb // 8)
-        ]
-        tiles = sweep_slab(tiles, r0, PIV, nb)
-        R = jnp.concatenate([jnp.concatenate(t, axis=1) for t in tiles], axis=0)
-        left = jnp.where(jnp.logical_and(lane >= r0, lane < r0 + nb), 0.0, slab)
-        lh, lm, ll = split3(left)
-        rh, rm, rl = split3(R)
-        la = jnp.concatenate([lh, lh, lm, lh, lm, ll], axis=0)
-        ra = jnp.concatenate([rh, rm, rh, rl, rm, rh], axis=0)
-        l0 = (r0 // 128) * 128
-        here = jnp.logical_and(cm >= r0 - l0, cm < r0 - l0 + nb)
-
-        def apply(a, z):
-            u = lax.dot_general(la[:, a:z], ra, TN, preferred_element_type=F32)
-            for lt in range(4):
-                cur = m_ref[a:z, 128 * lt : 128 * lt + 128]
-                if 128 * lt == l0:
-                    cur = jnp.where(here, 0.0, cur)
-                m_ref[a:z, 128 * lt : 128 * lt + 128] = cur - u[:, 128 * lt : 128 * lt + 128]
-
-        if k + 1 < count:
-            apply(r0 + nb, r0 + 2 * nb)
-            if r0 > 0:
-                apply(0, r0)
-            if r0 + 2 * nb < 256:
-                apply(r0 + 2 * nb, 256)
-        else:
-            apply(0, r0)
-        m_ref[r0 : r0 + nb, :] = R
+    r0 = k * nb
+    slab = m_ref[r0 : r0 + nb, 0:256]
+    tiles = [
+        [m_ref[r0 + 8 * rt : r0 + 8 * rt + 8, 128 * lt : 128 * lt + 128] for lt in range(4)]
+        for rt in range(nb // 8)
+    ]
+    tiles = sweep_slab(tiles, r0, PIV, nb)
+    R = jnp.concatenate([jnp.concatenate(t, axis=1) for t in tiles], axis=0)
+    left = jnp.where(jnp.logical_and(lane >= r0, lane < r0 + nb), 0.0, slab)
+    lh, lm, ll = split3(left)
+    rh, rm, rl = split3(R)
+    la = jnp.concatenate([lh, lh, lm, lh, lm, ll], axis=0)
+    ra = jnp.concatenate([rh, rm, rh, rl, rm, rh], axis=0)
+    l0 = (r0 // 128) * 128
+    here = jnp.logical_and(cm >= r0 - l0, cm < r0 - l0 + nb)
+
+    def apply(a, z):
+        u = lax.dot_general(la[:, a:z], ra, TN, preferred_element_type=F32)
+        for lt in range(4):
+            cur = m_ref[a:z, 128 * lt : 128 * lt + 128]
+            if 128 * lt == l0:
+                cur = jnp.where(here, 0.0, cur)
+            m_ref[a:z, 128 * lt : 128 * lt + 128] = cur - u[:, 128 * lt : 128 * lt + 128]
+
+    if r0 + nb < 256:
+        apply(r0 + nb, r0 + 2 * nb)
+    if r0 > 0:
+        apply(0, r0)
+    if r0 + 2 * nb < 256:
+        apply(r0 + 2 * nb, 256)
+    m_ref[r0 : r0 + nb, :] = R
+
+
+dot = functools.partial(lax.dot_general, dimension_numbers=NN, preferred_element_type=F32)
+exact = functools.partial(dot, precision=HI)
+GRP = 4
 
 
 def main_kernel(
@@ -384,19 +406,24 @@
     alon,
     diff,
     edge_ref,
+    ens,
     ext,
     out,
     rows_ref,
     x_ref,
+    reg_ref,
     mid_ref,
     o_ref,
     cb_ref,
     m_ref,
+    st_ref,
     sth_ref,
     stl_ref,
+    w_ref,
     wh_ref,
     wm_ref,
     wl_ref,
+    g_ref,
     u_ref,
     v_ref,
     insem,
@@ -404,8 +431,20 @@
 ):
     l = place[0]
     n = place[1]
-    load = pltpu.make_async_copy(ext, x_ref, insem)
-    load.start()
+    loads = [
+        pltpu.make_async_copy(src, x_ref.at[pl.ds(i, ni), pl.ds(j, nj)], insem.at[s])
+        for s, (src, i, ni, j, nj) in enumerate(
+            (
+                (ens, 2, CLAT, 2, CLON),
+                (ext.at[pl.ds(0, 2)], 0, 2, 0, CLON + 4),
+                (ext.at[pl.ds(CLAT + 2, 2)], CLAT + 2, 2, 0, CLON + 4),
+                (ext.at[pl.ds(2, CLAT), pl.ds(0, 2)], 2, CLAT, 0, 2),
+                (ext.at[pl.ds(2, CLAT), pl.ds(CLON + 2, 2)], 2, CLAT, CLON + 2, 2),
+            )
+        )
+    ]
+    for c in loads:
+        c.start()
     for b in range(NB):
         rows_ref[b] = rows_in[b]
 
@@ -418,20 +457,12 @@
             k - jnp.minimum(e, 0.0),
         )
 
-    def inner(q, carry):
-        i0 = q * 8
-        cells = [
-            jnp.transpose(r[pl.ds(i0, 8)].reshape(128, LEV)) for r in (alat, alon, diff)
-        ]
-        for f, d in enumerate(derived(*cells)):
-            for i in range(8):
-                for j in range(CLON):
-                    t = i * CLON + j
-                    cb_ref[f, i0 + 1 + i, 1 + j] = jnp.broadcast_to(d[:, t : t + 1], (8, 128))
-        return carry
-
-    lax.fori_loop(0, CLAT // 8, inner, 0)
-    for d in range(4):
+    def spread_column(j):
+        for f, d in enumerate(derived(alat[j], alon[j], diff[j])):
+            for i in range(CLAT):
+                cb_ref[f, 1 + i, 1 + j] = jnp.broadcast_to(d[:, i : i + 1], (8, 128))
+
+    def spread_edge(d):
         der = derived(edge_ref[d, 0], edge_ref[d, 1], edge_ref[d, 2])
         if d < 2:
             outside = (l == nlat - 1) if d == 0 else (l == 0)
@@ -439,15 +470,15 @@
         for f in range(5):
             w = der[f] * keep if d < 2 else der[f]
             for t in range(CLON if d < 2 else CLAT):
-                spread = jnp.broadcast_to(w[:, t : t + 1], (8, 128))
+                line = jnp.broadcast_to(w[:, t : t + 1], (8, 128))
                 if d == 0:
-                    cb_ref[f, CLAT + 1, 1 + t] = spread
+                    cb_ref[f, CLAT + 1, 1 + t] = line
                 elif d == 1:
-                    cb_ref[f, 0, 1 + t] = spread
+                    cb_ref[f, 0, 1 + t] = line
                 elif d == 2:
-                    cb_ref[f, 1 + t, CLON + 1] = spread
+                    cb_ref[f, 1 + t, CLON + 1] = line
                 else:
-                    cb_ref[f, 1 + t, 0] = spread
+                    cb_ref[f, 1 + t, 0] = line
 
     ri = lax.broadcasted_iota(jnp.int32, (256, 256), 0)
     ci = lax.broadcasted_iota(jnp.int32, (256, 256), 1)
@@ -459,8 +490,8 @@
 
     def where_obs(b):
         pos = lax.shift_right_logical(cells_ref[pl.ds(b, 1), :], 3)
-        lat = tiles_ref[b, 0] * CLAT + lax.shift_right_logical(pos, 4)
-        lon = tiles_ref[b, 1] * CLON + jnp.bitwise_and(pos, 15)
+        lat = tiles_ref[0, b] * CLAT + lax.shift_right_logical(pos, 4)
+        lon = tiles_ref[1, b] * CLON + jnp.bitwise_and(pos, 15)
         return lat.astype(F32), lon.astype(F32)
 
     def lon_sq(gap):
@@ -468,9 +499,7 @@
         gap = jnp.minimum(gap, total_lon - gap)
         return gap * gap
 
-    load.wait()
-
-    def batch(b, carry):
+    def prologue(b):
         rows = rows_ref[b]
         spread = rows - jnp.mean(rows, axis=1, keepdims=True)
         var = var_ref[pl.ds(b, 1), :]
@@ -482,64 +511,97 @@
             - rows
         )
         spread_t = jnp.transpose(spread) * (1.0 / (MEM - 1))
-        hi, lo = split2(spread_t)
-        sth_ref[...] = hi
-        stl_ref[...] = lo
-        eliminate(m_ref)
-        weights = m_ref[:, 256:512]
-        wh_ref[...], wm_ref[...], wl_ref[...] = split3(weights)
-
+        st_ref[...] = spread_t
+        sth_ref[...], stl_ref[...] = split2(spread_t)
         reach = radius_ref[b].astype(F32)
         inv_sq = 1.0 / (jnp.full((1, 256), 1.0, F32) * (reach * reach))
         obs_lat, obs_lon = where_obs(b)
-
-        def later(c, carry):
-            r = rows_ref[c]
-            mine_lat, mine_lon = where_obs(c)
-            dlat = column(mine_lat) - obs_lat
-            d2 = dlat * dlat + lon_sq(column(mine_lon) - obs_lon)
-            taper = jnp.maximum(1.0 - d2 * inv_sq, 0.0)
-            an = r - jnp.mean(r, axis=1, keepdims=True)
-            reg = lax.dot_general(an, spread_t, NN, precision=HI, preferred_element_type=F32)
-            reg = reg * (taper * taper)
-            rows_ref[c] = r + lax.dot_general(
-                reg, weights, NN, precision=HI, preferred_element_type=F32
-            )
-            return carry
-
-        lax.fori_loop(b + 1, NB, later, 0)
-
         for j in range(CLON + 4):
             pos = lax.rem(n * CLON + j - 2 + CLON * nlon, CLON * nlon).astype(F32)
             v_ref[j] = jnp.broadcast_to(lon_sq(pos - obs_lon) * inv_sq, (8, 256))
-
-        def lat_row(i, carry):
+        for i in range(CLAT + 4):
             gap = (l * CLAT + i - 2).astype(F32) - obs_lat
             u_ref[i] = jnp.broadcast_to(1.0 - gap * gap * inv_sq, (8, 256))
-            return carry
-
-        lax.fori_loop(0, CLAT + 4, lat_row, 0)
-
-        def block(i, carry):
-            x = x_ref[pl.ds(4 * i, 4)].reshape(4 * 20 * 8, 256)
-            an = x - jnp.mean(x, axis=1, keepdims=True)
-            ah, al = split2(an)
-            sh, sl = sth_ref[...], stl_ref[...]
-            dot = functools.partial(lax.dot_general, dimension_numbers=NN, preferred_element_type=F32)
-            reg = dot(ah, sh) + dot(al, sh) + dot(ah, sl)
-            tap = jnp.maximum(u_ref[pl.ds(4 * i, 4)][:, None] - v_ref[...][None], 0.0)
-            reg = reg * (tap * tap).reshape(4 * 20 * 8, 256)
-            gh, gm, gl = split3(reg)
-            wh, wm, wl = wh_ref[...], wm_ref[...], wl_ref[...]
-            small = dot(gm, wm) + dot(gh, wl) + dot(gl, wh)
-            x = x + (dot(gh, wh) + ((dot(gm, wh) + dot(gh, wm)) + small))
-            x_ref[pl.ds(4 * i, 4)] = x.reshape(4, 20, 8, 256)
-            return carry
-
-        lax.fori_loop(0, 9, block, 0)
+        return obs_lat, obs_lon, inv_sq
+
+    def regress_rows(c, where):
+        obs_lat, obs_lon, inv_sq = where
+        r = rows_ref[c]
+        mine_lat, mine_lon = where_obs(c)
+        dlat = column(mine_lat) - obs_lat
+        d2 = dlat * dlat + lon_sq(column(mine_lon) - obs_lon)
+        taper = jnp.maximum(1.0 - d2 * inv_sq, 0.0)
+        an = r - jnp.mean(r, axis=1, keepdims=True)
+        g_ref[c] = exact(an, st_ref[...]) * (taper * taper)
+
+    size = GRP * (CLON + 4) * LEV
+
+    def adjust(i):
+        at = pl.ds(GRP * i, GRP)
+        x = x_ref[at].reshape(size, MEM)
+        gh, gm, gl = split3(reg_ref[at].reshape(size, 256))
+        wh, wm, wl = wh_ref[...], wm_ref[...], wl_ref[...]
+        small = dot(gm, wm) + dot(gh, wl) + dot(gl, wh)
+        x = x + (dot(gh, wh) + ((dot(gm, wh) + dot(gh, wm)) + small))
+        x_ref[at] = x.reshape(GRP, CLON + 4, LEV, MEM)
+        return x
+
+    def regress(i, x=None):
+        at = pl.ds(GRP * i, GRP)
+        if x is None:
+            x = x_ref[at].reshape(size, MEM)
+        ah, al = split2(x - jnp.mean(x, axis=1, keepdims=True))
+        sh, sl = sth_ref[...], stl_ref[...]
+        reg = dot(ah, sh) + (dot(al, sh) + dot(ah, sl))
+        tap = jnp.maximum(u_ref[at][:, None] - v_ref[...][None], 0.0)
+        reg = reg * (tap * tap).reshape(size, 256)
+        reg_ref[at] = reg.reshape(GRP, CLON + 4, LEV, 256)
+
+    def keep_weights():
+        weights = m_ref[:, 256:512]
+        w_ref[...] = weights
+        wh_ref[...], wm_ref[...], wl_ref[...] = split3(weights)
+
+    where = prologue(0)
+    for c in loads:
+        c.wait()
+    for k in range(8):
+        panel(m_ref, k)
+        spread_column(2 * k)
+        spread_column(2 * k + 1)
+        if k < 4:
+            spread_edge(k)
+        regress(k)
+        if k == 7:
+            regress(8)
+        if k == 3:
+            regress_rows(1, where)
+        if k == 4:
+            regress_rows(2, where)
+    keep_weights()
+
+    def batch(b, carry):
+        rows_ref[b] = rows_ref[b] + exact(g_ref[b], w_ref[...])
+        where = prologue(b)
+        for k in range(8):
+            panel(m_ref, k)
+            regress(k, adjust(k))
+            if k == 7:
+                regress(8, adjust(8))
+            if k == 0:
+                rows_ref[2] = rows_ref[2] + exact(g_ref[2], w_ref[...])
+            if k == 3:
+                regress_rows(2, where)
+        keep_weights()
         return carry
 
-    lax.fori_loop(0, NB, batch, 0)
+    lax.fori_loop(1, NB, batch, 0)
+
+    def last(i, carry):
+        adjust(i)
+        return carry
+
+    lax.fori_loop(0, 9, last, 0)
 
     @pl.when(l == 0)
     def _():
@@ -578,6 +640,42 @@
 
     lax.fori_loop(0, CLAT, second, 0)
     pltpu.make_async_copy(o_ref, out, outsem).wait()
+
+
+def main_call(nlat, nlon):
+    dma = pltpu.SemaphoreType.DMA
+    sq = lambda t: pltpu.VMEM((256, 256), t)
+    return pl.pallas_call(
+        functools.partial(main_kernel, nlat, nlon),
+        out_shape=jax.ShapeDtypeStruct((CLAT, CLON, LEV, MEM), F32),
+        in_specs=[pl.BlockSpec(memory_space=SM)] * 3
+        + [pl.BlockSpec(memory_space=VM)] * 9
+        + [pl.BlockSpec(memory_space=pl.ANY)] * 2,
+        out_specs=pl.BlockSpec(memory_space=pl.ANY),
+        scratch_shapes=[
+            pltpu.VMEM((NB, NOBS, MEM), F32),
+            pltpu.VMEM((CLAT + 4, CLON + 4, LEV, MEM), F32),
+            pltpu.VMEM((CLAT + 4, CLON + 4, LEV, NOBS), F32),
+            pltpu.VMEM((CLAT + 2, CLON + 2, LEV, MEM), F32),
+            pltpu.VMEM((CLAT, CLON, LEV, MEM), F32),
+            pltpu.VMEM((5, CLAT + 2, CLON + 2, LEV, 128), F32),
+            pltpu.VMEM((256, 512), F32),
+            sq(F32),
+            sq(BF16),
+            sq(BF16),
+            sq(F32),
+            sq(BF16),
+            sq(BF16),
+            sq(BF16),
+            pltpu.VMEM((NB, 256, 256), F32),
+            pltpu.VMEM((CLAT + 4, LEV, 256), F32),
+            pltpu.VMEM((CLON + 4, LEV, 256), F32),
+            dma((5,)),
+            dma,
+        ],
+        compiler_params=pltpu.CompilerParams(vmem_limit_bytes=60 << 20),
+        name="assimilate",
+    )
 
 
 def shards(
@@ -594,54 +692,27 @@
     courant_lon,
     diffusivity,
 ):
-    l = lax.axis_index("lat")
-    n = lax.axis_index("lon")
-    own = jnp.logical_and(owner_tiles[:, 0] == l, owner_tiles[:, 1] == n).astype(F32)
-    place = jnp.stack([l, n]).astype(jnp.int32)
-
-    picked = pl.pallas_call(
-        pick_kernel,
-        out_shape=jax.ShapeDtypeStruct((NB, NOBS, MEM), F32),
-        in_specs=[
-            pl.BlockSpec(memory_space=SM),
-            pl.BlockSpec(memory_space=SM),
-            pl.BlockSpec(memory_space=VM),
-        ],
-        out_specs=pl.BlockSpec(memory_space=VM),
-        compiler_params=pltpu.CompilerParams(vmem_limit_bytes=24 << 20),
-        name="pick",
-    )(obs_cells, own, ensemble.reshape(-1, MEM))
-
-    coefs = jnp.stack([courant_lat, courant_lon, diffusivity])
-    pad = lambda x: jnp.pad(x, ((0, 0), (0, 0), (0, 32 - x.shape[2])))
-    edges = jnp.stack(
-        [
-            pad(jnp.swapaxes(coefs[:, 0], 1, 2)),
-            pad(jnp.swapaxes(coefs[:, CLAT - 1], 1, 2)),
-            jnp.swapaxes(coefs[:, :, 0], 1, 2),
-            jnp.swapaxes(coefs[:, :, CLON - 1], 1, 2),
-        ]
-    )
     piece = NOBS // nlon
     dma = pltpu.SemaphoreType.DMA
-    rows, edges_in, ext = pl.pallas_call(
+    tiles = owner_tiles.T
+    coefs = [jnp.transpose(c, (1, 2, 0)) for c in (courant_lat, courant_lon, diffusivity)]
+    vm = pl.BlockSpec(memory_space=VM)
+    sm = pl.BlockSpec(memory_space=SM)
+    anym = pl.BlockSpec(memory_space=pl.ANY)
+    rows, edges_in, place, ext = pl.pallas_call(
         functools.partial(exchange_kernel, nlat, nlon),
         out_shape=(
             jax.ShapeDtypeStruct((NB, NOBS, MEM), F32),
             jax.ShapeDtypeStruct((4, 3, LEV, 32), F32),
+            jax.ShapeDtypeStruct((2,), jnp.int32),
             jax.ShapeDtypeStruct((CLAT + 4, CLON + 4, LEV, MEM), F32),
         ),
-        in_specs=[
-            pl.BlockSpec(memory_space=VM),
-            pl.BlockSpec(memory_space=VM),
-            pl.BlockSpec(memory_space=pl.ANY),
-        ],
-        out_specs=(
-            pl.BlockSpec(memory_space=VM),
-            pl.BlockSpec(memory_space=VM),
-            pl.BlockSpec(memory_space=pl.ANY),
-        ),
+        in_specs=[sm, sm, anym, vm, vm, vm],
+        out_specs=(vm, vm, sm, anym),
         scratch_shapes=[
+            pltpu.VMEM((CLAT, CLON, LEV, MEM), F32),
+            pltpu.VMEM((NB, NOBS, MEM), F32),
+            pltpu.VMEM((4, 3, LEV, 32), F32),
             pltpu.VMEM((nlon - 1, NB, piece, MEM), F32),
             pltpu.VMEM((nlat - 1, NB, piece, MEM), F32),
             pltpu.VMEM((NB, piece, MEM), F32),
@@ -662,47 +733,20 @@
             collective_id=0, has_side_effects=True, vmem_limit_bytes=56 << 20
         ),
         name="exchange",
-    )(picked, edges, ensemble)
-
-    return pl.pallas_call(
-        functools.partial(main_kernel, nlat, nlon),
-        out_shape=jax.ShapeDtypeStruct((CLAT, CLON, LEV, MEM), F32),
-        in_specs=[pl.BlockSpec(memory_space=SM)] * 3
-        + [pl.BlockSpec(memory_space=VM)] * 9
-        + [pl.BlockSpec(memory_space=pl.ANY)],
-        out_specs=pl.BlockSpec(memory_space=pl.ANY),
-        scratch_shapes=[
-            pltpu.VMEM((NB, NOBS, MEM), F32),
-            pltpu.VMEM((CLAT + 4, CLON + 4, LEV, MEM), F32),
-            pltpu.VMEM((CLAT + 2, CLON + 2, LEV, MEM), F32),
-            pltpu.VMEM((CLAT, CLON, LEV, MEM), F32),
-            pltpu.VMEM((5, CLAT + 2, CLON + 2, LEV, 128), F32),
-            pltpu.VMEM((256, 512), F32),
-            pltpu.VMEM((256, 256), BF16),
-            pltpu.VMEM((256, 256), BF16),
-            pltpu.VMEM((256, 256), BF16),
-            pltpu.VMEM((256, 256), BF16),
-            pltpu.VMEM((256, 256), BF16),
-            pltpu.VMEM((CLAT + 4, LEV, 256), F32),
-            pltpu.VMEM((CLON + 4, LEV, 256), F32),
-            dma,
-            dma,
-        ],
-        compiler_params=pltpu.CompilerParams(vmem_limit_bytes=56 << 20),
-        name="assimilate",
-    )(
+    )(tiles, obs_cells, ensemble, *coefs)
+
+    return main_call(nlat, nlon)(
         place,
-        owner_tiles,
+        tiles,
         radius,
         rows,
         obs_noise,
         obs_values,
         obs_var,
         obs_cells,
-        courant_lat,
-        courant_lon,
-        diffusivity,
+        *coefs,
         edges_in,
+        ensemble,
         ext,
     )
 

time: 261 us -> 125 us (0.48)
  Pallas kernels: 246 us -> 123 us
  local copies, waits for them, and re-layouts: 10.7 us -> 0 us
  other arithmetic: 3.67 us -> 0 us
    pallas_call x1, Pallas kernels: 139 us -> 44.7 us  [shards(): pl.pallas_call(functools.partial(exchange_kernel, nlat, nlon), out_shape=...]
    pallas_call x2 -> x1, Pallas kernels: 107 us -> 78.1 us  [shards(): main_call(nlat, nlon)]
    unnamed x10 -> x0, local copies, waits for them, and re-layouts: 10.2 us -> none
    another operation x4 -> x0, other arithmetic: 2.91 us -> none  [the longest x2 1.41 us: shards(): jnp.stack([pad(jnp.swapaxes(coefs[:, 0], 1, 2)), pad(jnp.swapaxes(coefs[:...]
where the time goes in v2:
time: 125 us; the launch traced here: 123 us
  Pallas kernels  123 us (98%)
    pallas_call x1, Pallas kernels, shards(): main_call(nlat, nlon)  78.1 us
    pallas_call x1, Pallas kernels, shards(): pl.pallas_call(functools.partial(exchange_kernel, nlat, nlon), out_shape=...  44.7 us

profile of v2, /device:TPU:1, one launch (start us, length us, event | category | flops | bytes accessed | tf_op | source)
XLA Modules:
  0.0 123.0 jit_solution(16678431240502226914)
XLA Ops:
  0.0 44.7 %exchange.1 = (f32[3,256,256]{2,1,0:T(8,128)}, f32[4,3,8,32]{3,2,1,0:T(8,128)}, s32[2]{0:T(128)}, f32[36,20,8,256]{3,2,1,0:T(8,128)}) custom-call(s32[2,3]{1,0:T(2,128)} %bitcast.10, s32[3,256]{1,0:T(4,128)} %cells_ref.3, f32[32,16,8,256]{3,2,1,0:T(8,128)} %ens.3, f32[16,8,32]{2,1,0:T(8,128)} %bitcast.4, f32[16,8,32]{2,1,0:T(8,128)} %bitcast.6, ...), custom_call_target="tpu_custom_call" | custom-call | tf_op jit(solution)/shard_map/exchange/pallas_call | solution.py:702
  44.7 78.1 %assimilate.1 = f32[32,16,8,256]{3,2,1,0:T(8,128)} custom-call(s32[2]{0:T(128)} %get-tuple-element.9.place, s32[2,3]{1,0:T(2,128)} %bitcast.11, s32[3]{0:T(128)} %radius_ref.1, f32[3,256,256]{2,1,0:T(8,128)} %get-tuple-element.10.rows_in, f32[3,256,256]{2,1,0:T(8,128)} %noise_ref.1, f32[3,256]{1,0:T(4,128)} %values_ref.1, f32[3,256]{1,0:T(4,128)} %var_ref.1, ...), custom_call_target="tpu_custom_call" | custom-call | tf_op jit(solution)/shard_map/assimilate/pallas_call | solution.py:738

commit v3 on v2

--- a/solution.py
+++ b/solution.py
@@ -193,14 +193,6 @@
     pick(1)
     pick(2)
     send1(1)
-    wait1(0)
-    send2(0)
-    wait2(0)
-    send3(0)
-    wait1(1)
-    send2(1)
-    wait2(1)
-    send3(1)
 
     moves = (
         ((lm, n), (0, 2, 0, CLON), (34, 2)),
@@ -237,6 +229,16 @@
             )
     for c in copies:
         c.start()
+
+    wait1(0)
+    send2(0)
+    wait2(0)
+    send3(0)
+    wait1(1)
+    send2(1)
+    wait2(1)
+    send3(1)
+
     wait3(0)
     wait3(1)
     for g in range(2):
@@ -287,17 +289,24 @@
     return Q
 
 
-def sweep_slab(tiles, base, b, nrow):
+def sweep_slab(tiles, base, b, nrow, scr, hooks=()):
     rt_n, lt_n = nrow // 8, len(tiles[0])
     lane = lax.broadcasted_iota(jnp.int32, (8, 128), 1)
     sub = lax.broadcasted_iota(jnp.int32, (8, 128), 0)
     tiles = [list(r) for r in tiles]
     full = (8, 128)
+    piv = None
     for c in range(0, nrow, b):
         ltc, l0 = (base + c) // 128, (base + c) % 128
         rt0, s0 = c // 8, c % 8
+        o = (c // b) % 2 * 8
+        for lt in range(lt_n):
+            scr[o : o + 8, 128 * lt : 128 * lt + 128] = tiles[rt0][lt]
         rows = [
-            [jnp.broadcast_to(tiles[rt0][lt][s0 + s : s0 + s + 1, :], full) for lt in range(lt_n)]
+            [
+                jnp.broadcast_to(scr[o + s0 + s : o + s0 + s + 1, 128 * lt : 128 * lt + 128], full)
+                for lt in range(lt_n)
+            ]
             for s in range(b)
         ]
         cols = [
@@ -307,12 +316,35 @@
             ]
             for s in range(b)
         ]
-        p = {
-            (s, t): jnp.broadcast_to(rows[s][ltc][:, l0 + t : l0 + t + 1], full)
-            for s in range(b)
-            for t in range(s, b)
-        }
-        Q = inv_sym(p, b)
+        if piv is None:
+            piv = {
+                (s, t): jnp.broadcast_to(rows[s][ltc][:, l0 + t : l0 + t + 1], full)
+                for s in range(b)
+                for t in range(s, b)
+            }
+        Q = inv_sym(piv, b)
+        if c + b < nrow:
+            nl, n0 = (base + c + b) // 128, (base + c + b) % 128
+            rn, sn = (c + b) // 8, (c + b) % 8
+            X = {
+                (v, t): jnp.broadcast_to(rows[v][nl][:, n0 + t : n0 + t + 1], full)
+                for v in range(b)
+                for t in range(b)
+            }
+            nrows = [
+                jnp.broadcast_to(tiles[rn][nl][sn + s : sn + s + 1, :], full) for s in range(b)
+            ]
+            QX = {
+                (u, t): ssum(Q[u, v] * X[v, t] for v in range(b))
+                for u in range(b)
+                for t in range(b)
+            }
+            piv = {
+                (s, t): jnp.broadcast_to(nrows[s][:, n0 + t : n0 + t + 1], full)
+                - ssum(X[u, s] * QX[u, t] for u in range(b))
+                for s in range(b)
+                for t in range(s, b)
+            }
         colm = jnp.logical_and(lane >= l0, lane < l0 + b)
         R = []
         for s in range(b):
@@ -334,6 +366,8 @@
                     for s in range(b):
                         m = jnp.where(sub == s0 + s, R[s][lt], m)
                 tiles[rt][lt] = m
+        for hook in hooks[c // b :: nrow // b]:
+            hook()
     return tiles
 
 
@@ -349,7 +383,7 @@
     return h, (x - h.astype(F32)).astype(BF16)
 
 
-def panel(m_ref, k):
+def panel(m_ref, scr, k, hooks=()):
     nb = PANEL
     lane = lax.broadcasted_iota(jnp.int32, (nb, 256), 1)
     cm = lax.broadcasted_iota(jnp.int32, (1, 128), 1)
@@ -359,7 +393,7 @@
         [m_ref[r0 + 8 * rt : r0 + 8 * rt + 8, 128 * lt : 128 * lt + 128] for lt in range(4)]
         for rt in range(nb // 8)
     ]
-    tiles = sweep_slab(tiles, r0, PIV, nb)
+    tiles = sweep_slab(tiles, r0, PIV, nb, scr, hooks)
     R = jnp.concatenate([jnp.concatenate(t, axis=1) for t in tiles], axis=0)
     left = jnp.where(jnp.logical_and(lane >= r0, lane < r0 + nb), 0.0, slab)
     lh, lm, ll = split3(left)
@@ -416,6 +450,7 @@
     o_ref,
     cb_ref,
     m_ref,
+    scr,
     st_ref,
     sth_ref,
     stl_ref,
@@ -426,6 +461,8 @@
     g_ref,
     u_ref,
     v_ref,
+    g3_ref,
+    a2_ref,
     insem,
     outsem,
 ):
@@ -457,9 +494,9 @@
             k - jnp.minimum(e, 0.0),
         )
 
-    def spread_column(j):
+    def spread_column(j, i0, i1):
         for f, d in enumerate(derived(alat[j], alon[j], diff[j])):
-            for i in range(CLAT):
+            for i in range(i0, i1):
                 cb_ref[f, 1 + i, 1 + j] = jnp.broadcast_to(d[:, i : i + 1], (8, 128))
 
     def spread_edge(d):
@@ -546,16 +583,46 @@
         x_ref[at] = x.reshape(GRP, CLON + 4, LEV, MEM)
         return x
 
-    def regress(i, x=None):
+    def adjust_steps(i):
         at = pl.ds(GRP * i, GRP)
-        if x is None:
+        shape = (GRP, CLON + 4, LEV, MEM)
+
+        def parts():
+            g3_ref[0], g3_ref[1], g3_ref[2] = split3(reg_ref[at].reshape(size, 256))
+
+        def term(a, w):
+            x_ref[at] = x_ref[at] + dot(g3_ref[a], w[...]).reshape(shape)
+
+        pairs = ((0, wh_ref), (1, wh_ref), (0, wm_ref), (1, wm_ref), (0, wl_ref), (2, wh_ref))
+        return [parts] + [functools.partial(term, a, w) for a, w in pairs]
+
+    def regress_steps(i):
+        at = pl.ds(GRP * i, GRP)
+        shape = (GRP, CLON + 4, LEV, 256)
+
+        def parts():
             x = x_ref[at].reshape(size, MEM)
-        ah, al = split2(x - jnp.mean(x, axis=1, keepdims=True))
-        sh, sl = sth_ref[...], stl_ref[...]
-        reg = dot(ah, sh) + (dot(al, sh) + dot(ah, sl))
-        tap = jnp.maximum(u_ref[at][:, None] - v_ref[...][None], 0.0)
-        reg = reg * (tap * tap).reshape(size, 256)
-        reg_ref[at] = reg.reshape(GRP, CLON + 4, LEV, 256)
+            a2_ref[0], a2_ref[1] = split2(x - jnp.mean(x, axis=1, keepdims=True))
+            reg_ref[at] = dot(a2_ref[0], sth_ref[...]).reshape(shape)
+
+        def second():
+            reg_ref[at] = reg_ref[at] + dot(a2_ref[1], sth_ref[...]).reshape(shape)
+
+        def third():
+            reg = reg_ref[at] + dot(a2_ref[0], stl_ref[...]).reshape(shape)
+            tap = jnp.maximum(u_ref[at][:, None] - v_ref[...][None], 0.0)
+            reg_ref[at] = reg * (tap * tap)
+
+        return [parts, second, third]
+
+    def together(steps, count):
+        cut = [len(steps) * q // count for q in range(count + 1)]
+
+        def run(q):
+            for f in steps[cut[q] : cut[q + 1]]:
+                f()
+
+        return [functools.partial(run, q) for q in range(count)]
 
     def keep_weights():
         weights = m_ref[:, 256:512]
@@ -566,14 +633,14 @@
     for c in loads:
         c.wait()
     for k in range(8):
-        panel(m_ref, k)
-        spread_column(2 * k)
-        spread_column(2 * k + 1)
+        steps = regress_steps(k) + (regress_steps(8) if k == 7 else [])
+        hooks = together(steps, 8)
+        for q in range(8):
+            j = 2 * k + q // 4
+            hooks.append(functools.partial(spread_column, j, 8 * (q % 4), 8 * (q % 4) + 8))
+        panel(m_ref, scr, k, hooks)
         if k < 4:
             spread_edge(k)
-        regress(k)
-        if k == 7:
-            regress(8)
         if k == 3:
             regress_rows(1, where)
         if k == 4:
@@ -584,10 +651,10 @@
         rows_ref[b] = rows_ref[b] + exact(g_ref[b], w_ref[...])
         where = prologue(b)
         for k in range(8):
-            panel(m_ref, k)
-            regress(k, adjust(k))
+            steps = adjust_steps(k) + regress_steps(k)
             if k == 7:
-                regress(8, adjust(8))
+                steps += adjust_steps(8) + regress_steps(8)
+            panel(m_ref, scr, k, together(steps, 8))
             if k == 0:
                 rows_ref[2] = rows_ref[2] + exact(g_ref[2], w_ref[...])
             if k == 3:
@@ -660,6 +727,7 @@
             pltpu.VMEM((CLAT, CLON, LEV, MEM), F32),
             pltpu.VMEM((5, CLAT + 2, CLON + 2, LEV, 128), F32),
             pltpu.VMEM((256, 512), F32),
+            pltpu.VMEM((16, 512), F32),
             sq(F32),
             sq(BF16),
             sq(BF16),
@@ -670,6 +738,8 @@
             pltpu.VMEM((NB, 256, 256), F32),
             pltpu.VMEM((CLAT + 4, LEV, 256), F32),
             pltpu.VMEM((CLON + 4, LEV, 256), F32),
+            pltpu.VMEM((3, GRP * (CLON + 4) * LEV, 256), BF16),
+            pltpu.VMEM((2, GRP * (CLON + 4) * LEV, 256), BF16),
             dma((5,)),
             dma,
         ],

time: 125 us -> 116 us (0.928)
  Pallas kernels: 123 us -> 115 us
    pallas_call x1, Pallas kernels: 78.1 us -> 70.4 us  [shards(): main_call(nlat, nlon)]
where the time goes in v3:
time: 116 us; the launch traced here: 115 us
  Pallas kernels  115 us (99%)
    pallas_call x1, Pallas kernels, shards(): main_call(nlat, nlon)  70.4 us
    pallas_call x1, Pallas kernels, shards(): pl.pallas_call(functools.partial(exchange_kernel, nlat, nlon), out_shape=...  44.5 us

profile of v3, /device:TPU:1, one launch (start us, length us, event | category | flops | bytes accessed | tf_op | source)
XLA Modules:
  0.0 115.1 jit_solution(9901623739953199296)
XLA Ops:
  0.0 44.5 %exchange.1 = (f32[3,256,256]{2,1,0:T(8,128)}, f32[4,3,8,32]{3,2,1,0:T(8,128)}, s32[2]{0:T(128)}, f32[36,20,8,256]{3,2,1,0:T(8,128)}) custom-call(s32[2,3]{1,0:T(2,128)} %bitcast.10, s32[3,256]{1,0:T(4,128)} %cells_ref.3, f32[32,16,8,256]{3,2,1,0:T(8,128)} %ens.3, f32[16,8,32]{2,1,0:T(8,128)} %bitcast.4, f32[16,8,32]{2,1,0:T(8,128)} %bitcast.6, ...), custom_call_target="tpu_custom_call" | custom-call | tf_op jit(solution)/shard_map/exchange/pallas_call | solution.py:772
  44.6 70.4 %assimilate.1 = f32[32,16,8,256]{3,2,1,0:T(8,128)} custom-call(s32[2]{0:T(128)} %get-tuple-element.9.place, s32[2,3]{1,0:T(2,128)} %bitcast.11, s32[3]{0:T(128)} %radius_ref.1, f32[3,256,256]{2,1,0:T(8,128)} %get-tuple-element.10.rows_in, f32[3,256,256]{2,1,0:T(8,128)} %noise_ref.1, f32[3,256]{1,0:T(4,128)} %values_ref.1, f32[3,256]{1,0:T(4,128)} %var_ref.1, ...), custom_call_target="tpu_custom_call" | custom-call | tf_op jit(solution)/shard_map/assimilate/pallas_call | solution.py:808

commit v4 on v3

--- a/solution.py
+++ b/solution.py
@@ -43,16 +43,22 @@
     state,
     picked,
     edges,
+    got0,
+    halves,
     got1,
     got2,
     part1,
     part2,
+    s0,
+    r0,
     s1,
     r1,
     s2,
     r2,
     s3,
     r3,
+    s4,
+    r4,
     hs,
     hr,
     es,
@@ -62,6 +68,13 @@
     l = lax.axis_index("lat")
     n = lax.axis_index("lon")
     piece = NOBS // nlon
+    half = NOBS // 2
+    chips = nlon // 2
+    core, chip = lax.rem(n, 2), n // 2
+    twin = n + 1 - 2 * core
+    keep = pl.ds(pl.multiple_of(core * half, half), half)
+    give = pl.ds(pl.multiple_of((1 - core) * half, half), half)
+    mine = pl.ds(pl.multiple_of(core * half + chip * piece, piece), piece)
     lm, lp = lax.rem(l + nlat - 1, nlat), lax.rem(l + 1, nlat)
     nm, np_ = lax.rem(n + nlon - 1, nlon), lax.rem(n + 1, nlon)
 
@@ -112,22 +125,45 @@
 
     groups = ((0, 1), (1, 2))
 
+    def swap0(g):
+        b0, nb = groups[g]
+        return pltpu.make_async_remote_copy(
+            src_ref=picked.at[pl.ds(b0, nb), give],
+            dst_ref=got0.at[pl.ds(b0, nb)],
+            send_sem=s0.at[g],
+            recv_sem=r0.at[g],
+            device_id=(l, twin),
+            device_id_type=MESH,
+        )
+
+    def swap4(g):
+        b0, nb = groups[g]
+        return pltpu.make_async_remote_copy(
+            src_ref=rows.at[pl.ds(b0, nb), keep],
+            dst_ref=rows.at[pl.ds(b0, nb), keep],
+            send_sem=s4.at[g],
+            recv_sem=r4.at[g],
+            device_id=(l, twin),
+            device_id_type=MESH,
+        )
+
     def send1(g):
         b0, nb = groups[g]
+        halves[pl.ds(b0, nb)] = picked[pl.ds(b0, nb), keep, :] + got0[pl.ds(b0, nb)]
 
         def go(r, carry):
-            peer = lax.rem(n + r, nlon)
+            peer = lax.rem(chip + r, chips)
             pltpu.make_async_remote_copy(
-                src_ref=picked.at[pl.ds(b0, nb), pl.ds(peer * piece, piece)],
+                src_ref=halves.at[pl.ds(b0, nb), pl.ds(peer * piece, piece)],
                 dst_ref=got1.at[r - 1, pl.ds(b0, nb)],
                 send_sem=s1.at[g],
                 recv_sem=r1.at[g],
-                device_id=(l, peer),
+                device_id=(l, 2 * peer + core),
                 device_id_type=MESH,
             ).start()
             return carry
 
-        lax.fori_loop(1, nlon, go, 0)
+        lax.fori_loop(1, chips, go, 0)
 
     def wait1(g):
         b0, nb = groups[g]
@@ -136,8 +172,8 @@
 
     def send2(g):
         b0, nb = groups[g]
-        tot = picked[pl.ds(b0, nb), pl.ds(pl.multiple_of(n * piece, piece), piece), :]
-        for i in range(nlon - 1):
+        tot = halves[pl.ds(b0, nb), pl.ds(pl.multiple_of(chip * piece, piece), piece), :]
+        for i in range(chips - 1):
             tot = tot + got1[i, pl.ds(b0, nb)]
         part1[pl.ds(b0, nb)] = tot
 
@@ -166,34 +202,36 @@
         for i in range(nlat - 1):
             tot = tot + got2[i, pl.ds(b0, nb)]
         part2[pl.ds(b0, nb)] = tot
-        mine = pl.ds(pl.multiple_of(n * piece, piece), piece)
         rows[pl.ds(b0, nb), mine, :] = tot
 
         def go(r, carry):
-            peer = lax.rem(n + r, nlon)
+            peer = lax.rem(chip + r, chips)
             pltpu.make_async_remote_copy(
                 src_ref=part2.at[pl.ds(b0, nb)],
                 dst_ref=rows.at[pl.ds(b0, nb), mine],
                 send_sem=s3.at[g],
                 recv_sem=r3.at[g],
-                device_id=(l, peer),
+                device_id=(l, 2 * peer + core),
                 device_id_type=MESH,
             ).start()
             return carry
 
-        lax.fori_loop(1, nlon, go, 0)
+        lax.fori_loop(1, chips, go, 0)
 
     def wait3(g):
         b0, nb = groups[g]
-        full = rows.at[pl.ds(b0, nb), pl.ds(0, NOBS - piece)]
+        full = rows.at[pl.ds(b0, nb), pl.ds(0, half - piece)]
         pltpu.make_async_copy(full, full, r3.at[g]).wait()
 
+    firsts = [swap0(g) for g in range(2)]
+    lasts = [swap4(g) for g in range(2)]
     pick(0)
+    firsts[0].start()
+    pick(1)
+    firsts[0].wait_recv()
     send1(0)
-    pick(1)
     pick(2)
-    send1(1)
-
+    firsts[1].start()
     moves = (
         ((lm, n), (0, 2, 0, CLON), (34, 2)),
         ((lp, n), (CLAT - 2, 2, 0, CLON), (0, 2)),
@@ -232,6 +270,8 @@
 
     wait1(0)
     send2(0)
+    firsts[1].wait_recv()
+    send1(1)
     wait2(0)
     send3(0)
     wait1(1)
@@ -240,10 +280,16 @@
     send3(1)
 
     wait3(0)
+    lasts[0].start()
     wait3(1)
+    lasts[1].start()
+    for c in lasts:
+        c.wait_recv()
+    for c in firsts + lasts:
+        c.wait_send()
     for g in range(2):
         b0, nb = groups[g]
-        src = picked.at[pl.ds(b0, nb), pl.ds(0, NOBS - piece)]
+        src = halves.at[pl.ds(b0, nb), pl.ds(0, half - piece)]
         pltpu.make_async_copy(src, src, s1.at[g]).wait()
         full = got2.at[:, pl.ds(b0, nb)]
         pltpu.make_async_copy(full, full, s2.at[g]).wait()
@@ -783,10 +829,16 @@
             pltpu.VMEM((CLAT, CLON, LEV, MEM), F32),
             pltpu.VMEM((NB, NOBS, MEM), F32),
             pltpu.VMEM((4, 3, LEV, 32), F32),
-            pltpu.VMEM((nlon - 1, NB, piece, MEM), F32),
+            pltpu.VMEM((NB, NOBS // 2, MEM), F32),
+            pltpu.VMEM((NB, NOBS // 2, MEM), F32),
+            pltpu.VMEM((nlon // 2 - 1, NB, piece, MEM), F32),
             pltpu.VMEM((nlat - 1, NB, piece, MEM), F32),
             pltpu.VMEM((NB, piece, MEM), F32),
             pltpu.VMEM((NB, piece, MEM), F32),
+            dma((2,)),
+            dma((2,)),
+            dma((2,)),
+            dma((2,)),
             dma((2,)),
             dma((2,)),
             dma((2,)),

time: 116 us -> 115 us (level)
  no operation moved by 1% of the time
where the time goes in v4:
time: 115 us
  Pallas kernels  115 us (100%)
    pallas_call x1, Pallas kernels, shards(): main_call(nlat, nlon)  70.4 us
    pallas_call x1, Pallas kernels, shards(): pl.pallas_call(functools.partial(exchange_kernel, nlat, nlon), out_shape=...  44.2 us

profile of v4, /device:TPU:1, one launch (start us, length us, event | category | flops | bytes accessed | tf_op | source)
XLA Modules:
  0.0 114.8 jit_solution(3763772608701485576)
XLA Ops:
  0.0 44.2 %exchange.1 = (f32[3,256,256]{2,1,0:T(8,128)}, f32[4,3,8,32]{3,2,1,0:T(8,128)}, s32[2]{0:T(128)}, f32[36,20,8,256]{3,2,1,0:T(8,128)}) custom-call(s32[2,3]{1,0:T(2,128)} %bitcast.10, s32[3,256]{1,0:T(4,128)} %cells_ref.3, f32[32,16,8,256]{3,2,1,0:T(8,128)} %ens.3, f32[16,8,32]{2,1,0:T(8,128)} %bitcast.4, f32[16,8,32]{2,1,0:T(8,128)} %bitcast.6, ...), custom_call_target="tpu_custom_call" | custom-call | tf_op jit(solution)/shard_map/exchange/pallas_call | solution.py:818
  44.2 70.4 %assimilate.1 = f32[32,16,8,256]{3,2,1,0:T(8,128)} custom-call(s32[2]{0:T(128)} %get-tuple-element.9.place, s32[2,3]{1,0:T(2,128)} %bitcast.11, s32[3]{0:T(128)} %radius_ref.1, f32[3,256,256]{2,1,0:T(8,128)} %get-tuple-element.10.rows_in, f32[3,256,256]{2,1,0:T(8,128)} %noise_ref.1, f32[3,256]{1,0:T(4,128)} %values_ref.1, f32[3,256]{1,0:T(4,128)} %var_ref.1, ...), custom_call_target="tpu_custom_call" | custom-call | tf_op jit(solution)/shard_map/assimilate/pallas_call | solution.py:860
